TPU v7x, 128 devices: a whole 4x4x4 slice. The times are simulated.
128 devices in a mesh: row: 8 (over z_hi, y), col: 16 (over z_lo, x, core).
Axes of the slice: x: 4, y: 4, z: 4 (z_hi: 2, z_lo: 2; z = z_hi * 2 + z_lo), core: 2. Of those that a mesh axis runs over, the one named last changes fastest.
Arguments:
- features: bfloat16 [16, 8192, 256], P('col', 'row'), may hold values from -6 to 6
- adj_w: bfloat16 [8, 16, 320, 128, 128], P('row', 'col'), may hold values from -0.078125 to 0.078125
- row_of: int32 [8, 16, 320], P('row', 'col'), may hold values from 0 to 127
- col_of: int32 [8, 16, 320], P('row', 'col'), may hold values from 0 to 63
- live: int32 [8, 16], P('row', 'col'), may hold values from 80 to 320, as said below
- vid: int32 [8, 16384], P('row', 'col'), may hold values from 0 to 15
- w_in: bfloat16 [256, 512], replicated, may hold values from -0.375 to 0.375
- w_out: bfloat16 [512, 256], replicated, may hold values from -0.25 to 0.25
- cotangent: bfloat16 [8, 16384, 256], P('row', 'col'), may hold values from -6 to 6
Outputs:
- layer_out: bfloat16 [8, 16384, 256], P('row', 'col')
- grad_features: float32 [16, 8192, 256], P('col', 'row')
- grad_in: float32 [256, 512], replicated
- grad_out: float32 [512, 256], replicated
Inputs may be any that keep to these rules, and one draw needn't show every extreme that they name: `live`: some device uses all 320 slots.
All inputs are finite; a program needn't handle non-finite values.
Results may differ from a plain program's by a relative error of at most 0.025.
Values may be sent and summed in bfloat16 or wider, within the bound.
No kernel may reach another device: no remote copies, remote signals or barrier semaphores. Data moves between devices by JAX's collectives and lax.ppermute only.
A program may use at most 192 MiB of HBM per device.

v0:
```python
import math

import jax
import jax.numpy as jnp
from jax import lax
from jax.sharding import PartitionSpec as P

VN = 16


def shards(features, adj_w, row_of, col_of, live, vid, w_in, w_out, cotangent):
    n_row = lax.axis_size("row")
    n_col = lax.axis_size("col")
    blocks = adj_w[0, 0]
    target_idx = row_of[0, 0]
    source_idx = col_of[0, 0]
    kslots = blocks.shape[0]
    bsize = blocks.shape[1]
    width = features.shape[2]
    owned = features.shape[1] // bsize
    row_blocks = owned * n_col
    col_blocks = owned * n_row
    scale = math.sqrt(VN / (owned * bsize * n_row * n_col))
    keep = (jnp.arange(kslots) < live[0, 0]).astype(jnp.float32)[:, None, None]
    panel = lax.all_gather(features, "row", axis=1, tiled=True)
    source = panel.reshape(col_blocks, bsize, panel.shape[2])[source_idx]
    prods = jnp.einsum("kij,kjd->kid", blocks, source, preferred_element_type=jnp.float32) * keep
    part = jax.ops.segment_sum(prods, target_idx, num_segments=row_blocks)
    partial_value = part.astype(jnp.bfloat16).reshape(1, row_blocks * bsize, panel.shape[2])
    summed = lax.psum_scatter(
        partial_value.astype(jnp.float32).astype(jnp.bfloat16),
        "col",
        scatter_dimension=1,
        tiled=True,
    ).astype(jnp.float32)
    onehot = (jnp.arange(VN)[:, None] == vid[0][None, :]).astype(jnp.float32)
    local_pool = jnp.dot(onehot, summed[0], precision=lax.Precision.HIGHEST)
    pooled = lax.psum(local_pool, ("row", "col"))
    pooled = scale * pooled
    spread = jnp.einsum("vn,vd->nd", onehot, pooled, precision=lax.Precision.HIGHEST)
    mixed = (summed[0] + spread).astype(jnp.bfloat16)
    pre = jnp.dot(mixed, w_in, preferred_element_type=jnp.float32)
    hidden = jax.nn.silu(pre).astype(jnp.bfloat16)
    layer_out = (
        jnp.dot(hidden, w_out, preferred_element_type=jnp.float32) + mixed.astype(jnp.float32)
    ).astype(jnp.bfloat16)
    upstream = cotangent[0]
    local_out = jnp.einsum("nf,nd->fd", hidden, upstream, preferred_element_type=jnp.float32)
    grad_hidden = jnp.einsum("nd,fd->nf", upstream, w_out, preferred_element_type=jnp.float32)
    sig = jax.nn.sigmoid(pre)
    grad_pre = (grad_hidden * sig * (1.0 + pre * (1.0 - sig))).astype(jnp.bfloat16)
    local_in = jnp.einsum("nd,nf->df", mixed, grad_pre, preferred_element_type=jnp.float32)
    grad_mixed = jnp.einsum(
        "nf,df->nd", grad_pre, w_in, preferred_element_type=jnp.float32
    ) + upstream.astype(jnp.float32)
    local_grad_pool = jnp.dot(onehot, grad_mixed, precision=lax.Precision.HIGHEST)
    grad_pooled = scale * lax.psum(local_grad_pool, ("row", "col"))
    grad_in, grad_out = lax.psum((local_in, local_out), ("row", "col"))
    back_spread = jnp.einsum("vn,vd->nd", onehot, grad_pooled, precision=lax.Precision.HIGHEST)
    grad_summed = (grad_mixed + back_spread).astype(jnp.bfloat16)[None]
    grad_panel = lax.all_gather(grad_summed, "col", axis=1, tiled=True)
    target = grad_panel.reshape(row_blocks, bsize, width)[target_idx]
    prods = jnp.einsum("kij,kid->kjd", blocks, target, preferred_element_type=jnp.float32) * keep
    back = jax.ops.segment_sum(prods, source_idx, num_segments=col_blocks)
    back = back.astype(jnp.bfloat16).reshape(1, col_blocks * bsize, width)
    grad_features = lax.psum_scatter(
        back.astype(jnp.float32).astype(jnp.bfloat16), "row", scatter_dimension=1, tiled=True
    ).astype(jnp.float32)
    return (layer_out[None], grad_features, grad_in, grad_out)


def solution(mesh):
    in_specs = (
        P("col", "row", None),
        P("row", "col", None, None, None),
        P("row", "col", None),
        P("row", "col", None),
        P("row", "col"),
        P("row", "col"),
        P(),
        P(),
        P("row", "col", None),
    )
    out_specs = (P("row", "col", None), P("col", "row", None), P(), P())
    return jax.shard_map(shards, mesh=mesh, in_specs=in_specs, out_specs=out_specs, check_vma=False)
```

profile of v0, /device:TPU:1, one launch (start us, length us, event | category | flops | bytes accessed | tf_op | source)
XLA Modules:
  0.0 978.9 jit_solution(14377082108508796959)
XLA Ops:
  8.6 0.7 reduce
  9.3 0.7 fusion.21
  10.0 74.8 %all-gather.4.cloned.1.call-done = bf16[1,8192,256]{2,1,0:T(8,128)(2,1)} async-done(((bf16[1,1024,256]{2,1,0:T(8,128)(2,1)}), bf16[1,8192,256]{2,1,0:T(8,128)(2,1)}) %all-gather.4.cloned.1.call-update) | async-done | bytes 4194320 | tf_op jit(solution)/shard_map/all_gather | solution.py:25
  84.8 13.5 %gather_fusion = bf16[320,128,256]{2,1,0:T(8,128)(2,1)} fusion(bf16[64,128,256]{2,1,0:T(8,128)(2,1)} %bitcast.45, s32[1024]{0:T(1024)S(1)} %pad_clamp_fusion.1), kind=kCustom, calls=%fused_computation | custom fusion | bytes 41944320 | tf_op jit(solution)/shard_map/gather | solution.py:26
  98.3 31.3 %multiply_bitcast_fusion.1 = f32[320,128,256]{1,2,0:T(8,128)} fusion(f32[320]{0:T(512)S(1)} %fusion.20, bf16[320,128,256]{2,1,0:T(8,128)(2,1)} %gather_fusion, bf16[1,1,320,128,128]{4,3,2,1,0:T(8,128)(2,1)} %param.10), kind=kOutput, calls=%fused_computation.5 | convolution fusion | flops 2694840320 | bytes 73401600 | tf_op jit(solution)/shard_map/kij,kjd->kid/dot_general | solution.py:27
  129.6 41.6 %copy.16 = f32[320,128,256]{2,1,0:T(8,128)} copy(f32[320,128,256]{1,2,0:T(8,128)} %multiply_bitcast_fusion.1) | data formatting | bytes 83886080 | tf_op jit(solution)/shard_map/mul | solution.py:27
  171.3 7.8 broadcast_in_dim.16
  179.1 96.1 %scatter_fusion = f32[128,128,256]{2,1,0:T(8,128)} fusion(f32[128,128,256]{2,1,0:T(8,128)} %broadcast_in_dim.16, s32[320]{0:T(512)S(1)} %reduce, f32[320,128,256]{2,1,0:T(8,128)} %copy.16), kind=kCustom, calls=%fused_computation.2 | custom fusion | flops 10485760 | bytes 125830400 | tf_op jit(solution)/shard_map/scatter-add | solution.py:28
  275.2 9.0 convert_element_type.44
  284.3 68.6 %reduce-scatter.3.cloned.1.call-done = bf16[1,1024,256]{2,1,0:T(8,128)(2,1)} async-done(((bf16[1,16384,256]{2,1,0:T(8,128)(2,1)}), bf16[1,1024,256]{2,1,0:T(8,128)(2,1)}) %reduce-scatter.3.cloned.1.call-update) | async-done | bytes 524304 | tf_op jit(solution)/shard_map/reduce_scatter | solution.py:30
  353.0 1.2 fusion.9
  354.2 68.5 %psum.28 = f32[16,256]{1,0:T(8,128)S(1)} all-reduce(f32[16,256]{1,0:T(8,128)S(1)} %fusion.9), channel_id=1, replica_groups=mesh['row'=8,'col'=16] {'row','col'}, use_global_device_ids=true, to_apply=%region_2.0 | all-reduce | flops 4096 | bytes 32768 | tf_op jit(solution)/shard_map/psum | solution.py:38
  422.7 1.7 fusion.2
  424.4 1.7 multiply_convert_fusion.1
  426.1 0.9 multiply_convert_fusion
  428.0 62.6 %psum.29 = f32[16,256]{1,0:T(8,128)S(1)} all-reduce(f32[16,256]{1,0:T(8,128)S(1)} %fusion.11), channel_id=1, replica_groups=mesh['row'=8,'col'=16] {'row','col'}, use_global_device_ids=true, to_apply=%region_3.4 | all-reduce | flops 4096 | bytes 32768 | tf_op jit(solution)/shard_map/psum | solution.py:57
  490.6 1.4 fusion.3
  492.4 49.6 %all-gather.6.cloned.1.call-done = bf16[16384,256]{1,0:T(8,128)(2,1)} async-done(((bf16[1024,256]{1,0:T(8,128)(2,1)}), bf16[16384,256]{1,0:T(8,128)(2,1)}) %all-gather.6.cloned.1.call-update) | async-done | bytes 8388624 | tf_op jit(solution)/shard_map/all_gather | solution.py:61
  542.0 14.7 %gather_fusion.1 = bf16[320,128,256]{2,1,0:T(8,128)(2,1)} fusion(bf16[128,128,256]{2,1,0:T(8,128)(2,1)} %bitcast.46, s32[1024]{0:T(1024)S(1)} %pad_clamp_fusion), kind=kCustom, calls=%fused_computation.1 | custom fusion | bytes 41944320 | tf_op jit(solution)/shard_map/gather | solution.py:62
  556.7 27.5 %multiply_bitcast_fusion = f32[320,128,256]{1,2,0:T(8,128)} fusion(f32[320]{0:T(512)S(1)} %fusion.20, bf16[320,128,256]{2,1,0:T(8,128)(2,1)} %gather_fusion.1, bf16[1,1,320,128,128]{4,3,2,1,0:T(8,128)(2,1)} %param.10), kind=kOutput, calls=%fused_computation.4 | convolution fusion | flops 2694840320 | bytes 73401600 | tf_op jit(solution)/shard_map/kij,kid->kjd/dot_general | solution.py:63
  584.2 41.6 %copy.18 = f32[320,128,256]{2,1,0:T(8,128)} copy(f32[320,128,256]{1,2,0:T(8,128)} %multiply_bitcast_fusion) | data formatting | bytes 83886080 | tf_op jit(solution)/shard_map/mul | solution.py:63
  625.8 4.2 broadcast_in_dim.18
  630.0 94.9 %scatter_fusion.1 = f32[64,128,256]{2,1,0:T(8,128)} fusion(f32[64,128,256]{2,1,0:T(8,128)} %broadcast_in_dim.18, s32[320]{0:T(512)S(1)} %reduce.2, f32[320,128,256]{2,1,0:T(8,128)} %copy.18), kind=kCustom, calls=%fused_computation.3 | custom fusion | flops 10485760 | bytes 125830400 | tf_op jit(solution)/shard_map/scatter-add | solution.py:64
  724.9 6.0 convert_element_type.52
  731.0 1.3 fusion.25
  732.3 1.3 fusion.6
  733.6 2.2 fusion.5
  735.7 80.0 %reduce-scatter.5.cloned.1.call-done = bf16[1,1024,256]{2,1,0:T(8,128)(2,1)} async-done(((bf16[1,8192,256]{2,1,0:T(8,128)(2,1)}), bf16[1,1024,256]{2,1,0:T(8,128)(2,1)}) %reduce-scatter.5.cloned.1.call-update) | async-done | bytes 524304 | tf_op jit(solution)/shard_map/reduce_scatter | solution.py:66
  815.7 2.1 convert_element_type.53
  817.8 150.9 %all-reduce.3.cloned.1.call-done = (f32[256,512]{1,0:T(8,128)}, f32[512,256]{1,0:T(8,128)}) async-done(((f32[256,512]{1,0:T(8,128)}, f32[512,256]{1,0:T(8,128)}), (f32[256,512]{1,0:T(8,128)}, f32[512,256]{1,0:T(8,128)})) %all-reduce.3.cloned.1.call-update) | async-done | bytes 1048592 | tf_op jit(solution)/shard_map/psum | solution.py:58
  968.7 1.9 copy.26
  970.5 1.9 copy.27
  (33 shorter events, 2.2 us)
Async XLA Ops:
  7.2 417.2 %copy-start = (bf16[256,512]{1,0:T(8,128)(2,1)S(1)}, bf16[256,512]{1,0:T(8,128)(2,1)}, u32[]{:S(2)}) copy-start(bf16[256,512]{1,0:T(8,128)(2,1)} %param.15) | copy-start | bytes 786436
  7.2 77.6 %all-gather.4.cloned.1.call-start = ((), (), s32[]{:S(2)}) async-start(), calls=%async_computation.2 | async-start | bytes 4718592 | tf_op jit(solution)/shard_map/all_gather | solution.py:25
  7.9 345.0 %reduce-scatter.3.cloned.1.call-start = ((), (), s32[]{:S(2)}) async-start(), calls=%async_computation.3 | async-start | bytes 8912896 | tf_op jit(solution)/shard_map/reduce_scatter | solution.py:30
  275.2 77.7 %copy-start.5 = (s32[1,1024]{1,0:T(1,128)S(1)}, s32[1,1024]{1,0:T(1,128)}, u32[]{:S(2)}) copy-start(s32[1,1024]{1,0:T(1,128)} %param.14) | copy-start | bytes 12292
  284.3 141.9 %copy-start.3 = (bf16[1,1024,256]{2,1,0:T(8,128)(2,1)S(1)}, bf16[1,1024,256]{2,1,0:T(8,128)(2,1)}, u32[]{:S(2)}) copy-start(bf16[1,1024,256]{2,1,0:T(8,128)(2,1)} %param.17) | copy-start | bytes 1572868
  284.3 141.9 %copy-start.4 = (bf16[512,256]{1,0:T(8,128)(2,1)S(1)}, bf16[512,256]{1,0:T(8,128)(2,1)}, u32[]{:S(2)}) copy-start(bf16[512,256]{1,0:T(8,128)(2,1)} %param.16) | copy-start | bytes 786436
  284.3 257.7 %all-gather.6.cloned.1.call-start = ((), (), s32[]{:S(2)}) async-start(), calls=%async_computation.5 | async-start | bytes 8912896 | tf_op jit(solution)/shard_map/all_gather | solution.py:61
  426.1 66.2 %copy-start.6 = (s32[1,1,320]{2,1,0:T(1,128)S(1)}, s32[1,1,320]{2,1,0:T(1,128)}, u32[]{:S(2)}) copy-start(s32[1,1,320]{2,1,0:T(1,128)} %param.12) | copy-start | bytes 3844
  426.1 66.2 %copy-start.7 = (s32[1,1,320]{2,1,0:T(1,128)S(1)}, s32[1,1,320]{2,1,0:T(1,128)}, u32[]{:S(2)}) copy-start(s32[1,1,320]{2,1,0:T(1,128)} %param.11) | copy-start | bytes 3844
  492.0 323.7 %reduce-scatter.5.cloned.1.call-start = ((), (), s32[]{:S(2)}) async-start(), calls=%async_computation.4 | async-start | bytes 4718592 | tf_op jit(solution)/shard_map/reduce_scatter | solution.py:66
  724.9 7.4 copy-start.2
  724.9 247.5 %copy-start.1 = (bf16[256,512]{1,0:T(8,128)(2,1)S(1)}, bf16[256,512]{1,0:T(8,128)(2,1)}, u32[]{:S(2)}) copy-start(bf16[256,512]{1,0:T(8,128)(2,1)} %param.15) | copy-start | bytes 786436
  731.0 237.7 %all-reduce.3.cloned.1.call-start = ((), (), s32[]{:S(2)}) async-start(), calls=%async_computation.6 | async-start | bytes 2097152 | tf_op jit(solution)/shard_map/psum | solution.py:58
Sparse Core Ops, SparseCore 0:
  10.4 74.4 all-gather.3
  284.4 68.5 reduce-scatter.2
  492.1 49.8 all-gather.5
  731.1 84.5 reduce-scatter.4
  821.1 147.5 all-reduce.2
where the time goes:
time: 981 us; the launch traced here: 979 us
  waiting for transfers between devices  425 us (43%)
  other arithmetic  210 us (21%)
  blocking collectives  131 us (13%)
  local copies, waits for them, and re-layouts  127 us (13%)
  matrix products  71.3 us (7%)
  between operations  14.5 us (1%)
    psum x1, waiting for transfers between devices, shards(): grad_in, grad_out = lax.psum((local_in, local_out), ('row', 'col'))  151 us
    scatter-add x1, other arithmetic, shards(): part = jax.ops.segment_sum(prods, target_idx, num_segments=row_blocks)  96.1 us
    scatter-add x1, other arithmetic, shards(): back = jax.ops.segment_sum(prods, source_idx, num_segments=col_blocks)  94.9 us
    reduce_scatter x1, waiting for transfers between devices, shards(): lax.psum_scatter(back.astype(jnp.float32).astype(jnp.bfloat16), 'row', sc...  80 us
    all_gather x1, waiting for transfers between devices, shards(): panel = lax.all_gather(features, 'row', axis=1, tiled=True)  74.8 us
    reduce_scatter x1, waiting for transfers between devices, shards(): lax.psum_scatter(partial_value.astype(jnp.float32).astype(jnp.bfloat16),...  68.6 us
    psum x1, blocking collectives, shards(): pooled = lax.psum(local_pool, ('row', 'col'))  68.5 us
    psum x1, blocking collectives, shards(): grad_pooled = scale * lax.psum(local_grad_pool, ('row', 'col'))  62.6 us
  transfers between devices with their start and end apart: 5, of which 5 were waited for; matrix products, arithmetic and copies ran while one was open for 1% of the time, Pallas kernels for 0%

commit v1 on v0

v1 whole, which is shorter than its diff:
```python
import functools
import math

import jax
import jax.numpy as jnp
from jax import lax
from jax.experimental import pallas as pl
from jax.experimental.pallas import tpu as pltpu
from jax.sharding import PartitionSpec as P

VN = 16
BS = 128
UNROLL = 4
Q_UNROLL = 8
BOTH = ("row", "col")
MIB = 1 << 20
F32, BF16 = jnp.float32, jnp.bfloat16


def route(x=0, y=0, zl=0, zh=0, core=0):
    pairs = []
    for r in range(8):
        for c in range(16):
            to_r = ((r // 4 + zh) % 2) * 4 + (r % 4 + y) % 4
            to_c = ((c // 8 + zl) % 2) * 8 + ((c // 2 % 4 + x) % 4) * 2 + (c + core) % 2
            pairs.append((r * 16 + c, to_r * 16 + to_c))
    return pairs


def send(value, **step):
    return lax.ppermute(value, BOTH, route(**step))


def swap(value, axis, bit=1):
    stride = {"core": 1, "x": 2, "zl": 8, "y": 16, "zh": 64}[axis]
    return lax.ppermute(value, BOTH, [(i, i ^ (stride * bit)) for i in range(128)])


def tie(value, *before):
    return lax.optimization_barrier((value, before))[0]


def along(axis):
    if axis == "row":
        return (lambda v, s: send(v, y=s)), (lambda v: send(v, zh=1))
    return (lambda v, s: send(v, x=s)), (lambda v: send(v, zl=1))


def plus(*terms):
    total = terms[0].astype(F32)
    for term in terms[1:]:
        total = total + term.astype(F32)
    return total


def gather_first(axis, own):
    ring, pair = along(axis)
    return own, ring(own, -1), ring(own, 2), ring(own, 1), pair(own)


def scatter_first(axis, other):
    ring, pair = along(axis)
    return ring(other[1], 1), ring(other[3], -1), pair(other[2])


def scatter_add(own, other, got):
    r1, r3, z2 = got
    n = z2.shape[0]
    w2 = plus(own[2][:n], z2).astype(BF16)
    w2 = w2 if n == own[2].shape[0] else jnp.concatenate([w2, own[2][n:]])
    return plus(other[0], r1, r3).astype(BF16), w2


def scatter_last(axis, own, sums):
    ring, pair = along(axis)
    over, w2 = sums
    return own[0], ring(own[1], 1), ring(w2, 2), ring(own[3], -1), pair(over)


def add(value, *step):
    return value + swap(value, *step)


def place():
    r, c = lax.axis_index("row"), lax.axis_index("col")
    return r % 4, r // 4, c // 2 % 4, c // 8, c % 2


def merge(v, axis, place, bit=1):
    got = swap(v, axis, bit)
    return jnp.where(place & bit == 0, jnp.concatenate([v, got]), jnp.concatenate([got, v]))


def halve(v, place):
    n = v.shape[0] // 2
    take = lambda i: lax.dynamic_slice_in_dim(v, i * n, n)
    return take(place), take(1 - place).astype(BF16)


def agree(weights, pool, *step):
    terms = jnp.concatenate([weights.astype(BF16), *split(pool)])
    total = terms.astype(F32) + swap(terms, *step).astype(F32)
    n = weights.shape[0]
    return total[:n], total[n : n + VN] + total[n + VN :]


def dot(a, b, ca=1, cb=0):
    return lax.dot_general(a, b, (((ca,), (cb,)), ((), ())), preferred_element_type=F32)


def split(v):
    hi = v.astype(BF16)
    return hi, (v - hi.astype(F32)).astype(BF16)


def onehot_of(ids):
    rows = lax.broadcasted_iota(jnp.int32, (VN, ids.shape[-1]), 0)
    return (rows == ids).astype(F32).astype(BF16)


def fast(v):
    return pltpu.with_memory_space_constraint(v, pltpu.VMEM)


def call(kernel, scalars, operands, outs, scratch=(), flops=0, moved=0, left=0):
    vmem = pl.BlockSpec(memory_space=pltpu.VMEM)
    return pl.pallas_call(
        kernel,
        out_shape=[pltpu.VMEM(shape, dtype) for shape, dtype in outs],
        grid_spec=pltpu.PrefetchScalarGridSpec(
            num_scalar_prefetch=len(scalars),
            grid=(),
            in_specs=[pl.BlockSpec(memory_space=pl.ANY)] * left + [vmem] * (len(operands) - left),
            out_specs=[vmem] * len(outs),
            scratch_shapes=list(scratch),
        ),
        compiler_params=pltpu.CompilerParams(vmem_limit_bytes=8 * MIB),
        cost_estimate=pl.CostEstimate(flops=flops, bytes_accessed=moved, transcendentals=0),
    )(*scalars, *operands[:left], *[fast(v) for v in operands[left:]])


def slow(v):
    return pltpu.with_memory_space_constraint(v, pltpu.HBM)


def block(i):
    return pl.ds(pl.multiple_of(i * BS, BS), BS)


def q_kernel(src, dst, live, stored, ids, out, adj, acc, sems):
    parts = sems.shape[0]
    n = adj.shape[0] // parts
    copies = [pltpu.make_async_copy(stored.at[pl.ds(i * n, n)], adj.at[pl.ds(i * n, n)], sems.at[i]) for i in range(parts)]
    for copy in copies:
        copy.start()
    acc[...] = jnp.zeros_like(acc)
    for part, copy in enumerate(copies):
        copy.wait()

        def step(i, carry):
            for u in range(Q_UNROLL):
                k = part * n + i * Q_UNROLL + u
                acc[:, block(src[k])] += dot(onehot_of(ids[dst[k]]), adj[k])
            return carry

        here = jnp.clip(live[0] - part * n, 0, n)
        lax.fori_loop(0, (here + Q_UNROLL - 1) // Q_UNROLL, step, 0)
    hi, lo = split(acc[:, : out.shape[1]])
    out[0:VN] = hi
    out[VN : 2 * VN] = lo


def source_kernel(q, *refs):
    shards, (panel, pool) = refs[:8], refs[8:]
    nodes = shards[0].shape[0]
    for spot, ref in enumerate(shards):
        panel[pl.ds(spot * nodes, nodes)] = ref[...]
    panel[pl.ds(8 * nodes, BS)] = jnp.zeros((BS, panel.shape[1]), BF16)
    total = jnp.zeros((2 * VN, panel.shape[1]), F32)
    deep = 1024
    for i in range(q.shape[1] // deep):
        rows = pl.ds(i * deep, deep)
        total += dot(q[0 : 2 * VN, rows], panel[rows])
    pool[...] = total[:VN] + total[VN:]


def target_kernel(adj, *refs):
    shards, near, far, (panel, adj_out, sem, sems) = refs[:8], refs[8], refs[9:12], refs[12:]
    load = pltpu.make_async_copy(adj, adj_out, sem)
    load.start()
    nodes = shards[0].shape[0]
    moves = [(ref, 0, spot, 1) for spot, ref in enumerate(shards)] + [(near, 0, 8, 5)]
    moves += [(ref, 0, 13 + i, 1) for i, ref in enumerate(far)]
    copies = []
    for ref, at, spot, n in moves:
        to = panel.at[pl.ds(spot * nodes, n * nodes)]
        copies.append(pltpu.make_async_copy(ref.at[pl.ds(at, n * nodes)], to, sems.at[len(copies)]))
    for copy in copies:
        copy.start()
    panel[pl.ds(16 * nodes, BS)] = jnp.zeros((BS, panel.shape[1]), BF16)
    for copy in copies:
        copy.wait()
    load.wait()


def final_kernel(gp, *refs):
    terms, out = refs[:-1], refs[-1]
    hi, lo = split(gp[...])
    nodes = out.shape[0]
    width = out.shape[1]
    for k in range(nodes // width):
        rows, ride = pl.ds(k * width, width), pl.ds(nodes + k * VN, VN)
        q = plus(*[t[ride] for t in terms]).astype(BF16)
        out[rows] = plus(*[t[rows] for t in terms]) + dot(q, hi, 0, 0) + dot(q, lo, 0, 0)


def pairs_kernel(backward, low, high, c0, c1, to, ends, adj, panel, *refs):
    width = panel.shape[1]
    zero = panel.shape[0] // BS - 1
    first_pair, last = ends[low], ends[high]
    out = refs[-1]
    begin = low * (out.shape[0] // BS // (high - low))

    def step(i, acc):
        for u in range(UNROLL):
            p = first_pair + i * UNROLL + u
            real = p < last
            p = jnp.minimum(p, last - 1)
            e0, e1, t = c0[p], c1[p], to[p]
            x0 = panel[block(jnp.where(real, e0 & 255, zero))]
            x1 = panel[block(jnp.where(real, e1 & 255, zero))]
            side = 0 if backward else 1
            lhs = jnp.concatenate([adj[e0 >> 8], adj[e1 >> 8]], axis=side)
            prod = dot(lhs, jnp.concatenate([x0, x1], axis=0), side, 0)
            fresh = jnp.logical_and(real, (t & 1) == 1)
            acc = prod + jnp.where(fresh, jnp.zeros_like(acc), acc)
            out[block((t >> 1) - begin)] = acc.astype(BF16)
        return acc

    steps = (last - first_pair + UNROLL - 1) // UNROLL
    lax.fori_loop(0, steps, step, jnp.zeros((BS, width), F32))
    if backward:
        q, pieces = refs[0], refs[1:-1]
        nodes = out.shape[0] // 4
        for spot, piece in enumerate(pieces):
            piece[pl.ds(0, nodes)] = out[pl.ds(spot * nodes, nodes)]
            for k in range(nodes // width):
                piece[pl.ds(nodes + k * VN, VN)] = q[0:VN, pl.ds(((low * 4 + spot) * 4 + k) * width, width)]


def plan(used, to, frm, n_to, zero, parts):
    kslots = used.shape[0]
    n_pairs = kslots // 2 + n_to
    k = jnp.arange(kslots)
    key = jnp.where(used, to, -1)
    d = jnp.arange(n_to)
    rank = jnp.sum((key[:, None] == key[None, :]) & (k[None, :] < k[:, None]), axis=1)
    count = jnp.sum(key[None, :] == d[:, None], axis=1)
    need = jnp.maximum(1, (count + 1) // 2)
    offset = jnp.sum(jnp.where(d[None, :] < d[:, None], need[None, :], 0), axis=1)
    base = jnp.sum(jnp.where(key[:, None] == d[None, :], offset[None, :], 0), axis=1)
    spot = jnp.where(used, 2 * base + rank, -1)
    p = jnp.arange(2 * n_pairs)
    code = zero + jnp.sum(jnp.where(p[:, None] == spot[None, :], (k * 256 + frm - zero)[None, :], 0), axis=1)
    code = code.reshape(n_pairs, 2).astype(jnp.int32)
    p = jnp.arange(n_pairs)
    at = jnp.sum(offset[None, :] <= p[:, None], axis=1) - 1
    first = jnp.sum(offset[None, :] == p[:, None], axis=1)
    ends = jnp.stack([offset[i * n_to // parts] for i in range(parts)] + [jnp.sum(need)]).astype(jnp.int32)
    return code[:, 0], code[:, 1], (2 * at + first).astype(jnp.int32), ends


def mlp_kernel(ids, pooled, w_in, w_out, cot, *refs):
    terms, (mixed_out, hidden_out, grad_pre_out, grad, pool) = refs[:5], refs[5:]
    p_hi, p_lo = split(pooled[...])
    tile = 256
    total = jnp.zeros(pooled.shape, F32)
    for i in range(cot.shape[0] // tile):
        rows = pl.ds(i * tile, tile)
        hot = onehot_of(ids[:, rows])
        spread = dot(hot, p_hi, 0, 0) + dot(hot, p_lo, 0, 0)
        mixed = (plus(*[t[rows] for t in terms]) + spread).astype(BF16)
        pre = dot(mixed, w_in[...])
        sig = jax.nn.sigmoid(pre)
        hidden_out[rows] = (pre * sig).astype(BF16)
        grad_hidden = dot(cot[rows], w_out[...], 1, 1)
        grad_pre = (grad_hidden * sig * (1.0 + pre * (1.0 - sig))).astype(BF16)
        hi, lo = split(dot(grad_pre, w_in[...], 1, 1) + cot[rows].astype(F32))
        total += dot(hot, hi) + dot(hot, lo)
        grad[rows] = hi
        mixed_out[rows] = mixed
        grad_pre_out[rows] = grad_pre
    pool[pl.ds(0, VN)], pool[pl.ds(VN, VN)] = split(total)


def mlp(vid, pooled, w_in, w_out, cot, parts):
    rows, width = cot.shape
    hidden = w_in.shape[1]
    return call(
        mlp_kernel, (), [vid, pooled, w_in, w_out, cot, *parts],
        [((rows, width), BF16), ((rows, hidden), BF16), ((rows, hidden), BF16), ((rows, width), BF16), ((2 * VN, width), BF16)],
        (), 6 * rows * width * hidden, 8 * rows * width,
    )


def shards(features, adj_w, row_of, col_of, live, vid, w_in, w_out, cotangent):
    adj = adj_w[0, 0]
    kslots = adj.shape[0]
    nodes, width = features.shape[1:]
    owned = nodes // BS
    scale = math.sqrt(VN / (nodes * 128))
    y, zh, x, zl, core = place()
    used = jnp.arange(kslots) < live[0, 0]
    tgt, src = row_of[0, 0], col_of[0, 0]
    far = tgt // owned
    near = (((far % 2) ^ core) * 2 + ((far // 8) ^ zl)) * 4 + (far // 2 - x) % 4
    dst_blocks = 16 * owned
    src_blocks = 8 * owned
    dst = jnp.where(used, near * owned + tgt % owned, dst_blocks).astype(jnp.int32)
    home = src // owned
    at = (((home // 4) ^ zh) * 4 + (home - y) % 4) * owned + src % owned
    src = jnp.where(used, at, src_blocks).astype(jnp.int32)
    tgt_read = jnp.where(used, tgt, 0)
    count = live[0]
    to_dst = plan(used, dst, src, dst_blocks, src_blocks, 4)
    to_src = plan(used, src, dst, src_blocks, dst_blocks, 2)
    part = width
    flops = 2 * kslots * BS * BS * part

    ring, pair = along("row")
    own, a1, a2, a3, b0 = gather_first("row", features[0])
    stored = slow(adj)
    ids = merge(merge(vid[0][None], "core", core), "x", x, 1)
    ids = merge(merge(ids, "x", x, 2), "zl", zl).reshape(dst_blocks, 1, BS)
    a2, ids = tie((a2, ids), to_dst, to_src)
    b1, b2, b3 = ring(b0, -1), pair(a2), ring(b0, 1)
    q, adj = call(
        q_kernel, (src, tgt_read, count), [stored, ids], [((2 * VN, src_blocks * BS), BF16), (adj.shape, BF16)],
        [pltpu.VMEM((VN, (src_blocks + 1) * BS), F32), pltpu.SemaphoreType.DMA((5,))],
        2 * kslots * BS * BS * VN, adj.size * 2, 1,
    )
    pieces = [own, a1, a2, a3, b0, *tie((b1, b2, b3), q)]
    panel, pool = call(
        source_kernel, (), [q, *pieces], [(((src_blocks + 1) * BS, part), BF16), ((VN, part), F32)]
    )

    def forward(low, high, panel):
        return call(
            functools.partial(pairs_kernel, False, low, high), to_dst, [adj, panel],
            [((dst_blocks // 4 * (high - low) * BS, part), BF16)], (), flops // 2, adj.size,
        )[0]

    give = forward(2, 4, panel)
    pool, panel = tie((add(pool, "zl"), panel), give)
    got = send(give, core=1)
    keep_o = forward(1, 2, panel)
    pool, keep_o = tie((add(pool, "zh"), keep_o))
    piece = lambda keep, at, i: plus(keep[i * nodes : i * nodes + nodes], got[(at + i) * nodes : (at + i + 1) * nodes]).astype(BF16)
    other = [piece(keep_o, 4, i) for i in range(4)]
    o = scatter_first("col", other)
    pool, panel = tie((pool, panel), other)
    keep_w = forward(0, 1, panel)
    pool, keep_w = tie((add(pool, "y"), keep_w))
    pool, keep_w, o = tie((add(add(pool, "y", 2), "core"), keep_w, o))
    rider = jnp.concatenate(split(pool))
    own = [jnp.concatenate([piece(keep_w, 0, i), rider]) for i in range(4)]
    parts = scatter_last("col", own, scatter_add(own, other, o))
    riders = [p[nodes:] for p in parts[:4]]
    pooled = scale * plus(*[r[:VN] for r in riders], *[r[VN:] for r in riders])

    mixed, hidden, grad_pre, grad, pool = mlp(vid, pooled, w_in, w_out, cotangent[0], parts)
    ring, pair = along("col")
    own, a1, a2, a3, b0 = gather_first("col", grad)
    weights = jnp.concatenate([dot(grad_pre, mixed, 0, 0), dot(hidden, cotangent[0], 0, 0)])
    layer_out = (dot(hidden, w_out) + mixed.astype(F32)).astype(BF16)
    fan = w_in.shape[1]
    quads = weights.reshape(4, fan // 2, width)
    w0, w1, w2, w3 = [lax.dynamic_index_in_dim(quads, (x + k) % 4, 0, keepdims=False).astype(BF16) for k in range(4)]
    a2, b0 = tie((a2, b0), layer_out, w1, w2, w3)
    b1 = ring(jnp.concatenate([b0, w3, pool]), -1)
    b3 = ring(jnp.concatenate([b0, w1, pool]), 1)
    b2 = pair(a2)
    near = send(jnp.concatenate([own, a1, a2, a3, b0]), core=1)
    terms = jnp.concatenate([w0, pool]), ring(jnp.concatenate([w2, pool]), 2), b1[nodes:], b3[nodes:]
    terms = plus(*terms)
    deep = fan // 2
    weights, pool = terms[:deep], terms[deep : deep + VN] + terms[deep + VN :]
    far = [send(b, core=1) for b in (b1, b2, b3)]
    weights, pool = agree(weights, pool, "y")
    panel, adj = call(
        target_kernel, (), [stored, own, a1, a2, a3, b0, b1, b2, b3, near, *far],
        [(((dst_blocks + 1) * BS, part), BF16), (stored.shape, BF16)],
        [pltpu.SemaphoreType.DMA, pltpu.SemaphoreType.DMA((12,))], 0, stored.size * 2, 13,
    )
    weights, pool, panel = tie((weights, pool, panel))

    ride = nodes // width * VN
    outs = [((nodes + ride, part), BF16)] * 4

    def backward(low, panel):
        return call(
            functools.partial(pairs_kernel, True, low, low + 1), to_src, [adj, panel, q],
            outs, [pltpu.VMEM((src_blocks // 2 * BS, part), BF16)], flops // 2, adj.size,
        )

    other = backward(1, panel)
    weights, pool, other = tie((*agree(weights, pool, "zh"), other))
    o = scatter_first("row", other)
    own = backward(0, panel)
    weights, pool, own, o = tie((*agree(weights, pool, "y", 2), own, o))
    sums = scatter_add(own, other, o)
    weights, pool = tie((weights, pool), sums)
    terms = scatter_last("row", own, sums)
    weights, pool = agree(*agree(weights, pool, "core"), "zl")
    weights = tie(weights.astype(BF16), terms[-1])
    for bit in (1, 2):
        weights = merge(weights, "x", x, bit)
    grad_features = pl.pallas_call(
        final_kernel, out_shape=jax.ShapeDtypeStruct((nodes, part), F32)
    )(scale * pool, *terms)
    grad_in = weights[:fan].astype(F32).T
    grad_out = weights[fan:].astype(F32)
    return (layer_out[None], grad_features[None], grad_in, grad_out)


def solution(mesh):
    in_specs = (
        P("col", "row", None),
        P("row", "col", None, None, None),
        P("row", "col", None),
        P("row", "col", None),
        P("row", "col"),
        P("row", "col"),
        P(),
        P(),
        P("row", "col", None),
    )
    out_specs = (P("row", "col", None), P("col", "row", None), P(), P())
    return jax.shard_map(shards, mesh=mesh, in_specs=in_specs, out_specs=out_specs, check_vma=False)
```

time: 981 us -> 253 us (0.26)
  waiting for transfers between devices: 425 us -> 106 us
  other arithmetic: 210 us -> 13.4 us
  blocking collectives: 131 us -> 0 us
  local copies, waits for them, and re-layouts: 127 us -> 9.36 us
  starting transfers between devices: 0.42 us -> 76.5 us
  matrix products: 71.3 us -> 2.2 us
  Pallas kernels: 0 us -> 42.6 us
  between operations: 14.5 us -> 2.08 us
    scatter-add x2 -> x0, other arithmetic: 191 us -> none  [the longest x1 96.1 us: shards(): part = jax.ops.segment_sum(prods, target_idx, num_segments=row_blocks)]
    psum x1 -> x0, waiting for transfers between devices: 151 us -> none  [shards(): grad_in, grad_out = lax.psum((local_in, local_out), ('row', 'col'))]
    reduce_scatter x2 -> x0, waiting for transfers between devices: 149 us -> none  [the longest x1 80 us: shards(): lax.psum_scatter(back.astype(jnp.float32).astype(jnp.bfloat16), 'row', sc...]
    psum x2 -> x0, blocking collectives: 131 us -> none  [the longest x1 68.5 us: shards(): pooled = lax.psum(local_pool, ('row', 'col'))]
    all_gather x2 -> x0, waiting for transfers between devices: 124 us -> none  [the longest x1 74.8 us: shards(): panel = lax.all_gather(features, 'row', axis=1, tiled=True)]
    ppermute x0 -> x50, waiting for transfers between devices: none -> 106 us  [the longest x34 80.9 us: send(): return lax.ppermute(value, BOTH, route(**step))]
    mul x2 -> x0, local copies, waits for them, and re-layouts: 83.3 us -> none  [the longest x1 41.6 us: shards(): jnp.einsum('kij,kjd->kid', blocks, source, preferred_element_type=jnp.flo...]
    ppermute x0 -> x50, starting transfers between devices: none -> 76.5 us  [the longest x34 49.8 us: send(): return lax.ppermute(value, BOTH, route(**step))]
  transfers between devices with their start and end apart: 5 -> 50, of which waited for: 5 -> 20; matrix products, arithmetic and copies ran while one was open for 1% -> 7% of each run, Pallas kernels for 0% -> 11%
where the time goes in v1:
time: 253 us
  waiting for transfers between devices  106 us (42%)
  starting transfers between devices  76.5 us (30%)
  Pallas kernels  42.6 us (17%)
  other arithmetic  13.4 us (5%)
  local copies, waits for them, and re-layouts  9.36 us (4%)
    ppermute x34, waiting for transfers between devices, send(): return lax.ppermute(value, BOTH, route(**step))  80.9 us
    ppermute x34, starting transfers between devices, send(): return lax.ppermute(value, BOTH, route(**step))  49.8 us
    pallas_call x9, Pallas kernels, call(): pl.pallas_call(kernel, out_shape=[pltpu.VMEM(shape, dtype) for shape, dty...  39.4 us
    ppermute x16, starting transfers between devices, swap(): lax.ppermute(value, BOTH, [(i, i ^ stride * bit) for i in range(128)])  26.7 us
    ppermute x16, waiting for transfers between devices, swap(): lax.ppermute(value, BOTH, [(i, i ^ stride * bit) for i in range(128)])  25.5 us
  transfers between devices with their start and end apart: 50, of which 20 were waited for; matrix products, arithmetic and copies ran while one was open for 7% of the time, Pallas kernels for 11%

profile of v1, /device:TPU:1, one launch (start us, length us, event | category | flops | bytes accessed | tf_op | source)
XLA Modules:
  0.0 252.6 jit_solution(17635131258171250301)
XLA Ops:
  0.6 4.5 %collective-permute-start.7 = (bf16[1024,256]{1,0:T(8,128)(2,1)}, bf16[1024,256]{1,0:T(8,128)(2,1)S(1)}, u32[]{:S(2)}, u32[]{:S(2)}) collective-permute-start(bf16[1024,256]{1,0:T(8,128)(2,1)} %bitcast.32), channel_id=1, source_target_pairs={{0,64},{1,65},{2,66},{3,67},{4,68},{5,69},{6,70},{7,71},{8,72},{9,... | collective-permute-start | bytes 1572872 | tf_op jit(solution)/shard_map/ppermute | solution.py:31
  5.1 2.9 %collective-permute-start = (bf16[1024,256]{1,0:T(8,128)(2,1)}, bf16[1024,256]{1,0:T(8,128)(2,1)S(1)}, u32[]{:S(2)}, u32[]{:S(2)}) collective-permute-start(bf16[1024,256]{1,0:T(8,128)(2,1)} %bitcast.33), channel_id=1, source_target_pairs={{0,32},{1,33},{2,34},{3,35},{4,36},{5,37},{6,38},{7,39},{8,40},{9,... | collective-permute-start | bytes 1572872 | tf_op jit(solution)/shard_map/ppermute | solution.py:31
  19.2 2.8 %collective-permute-start.3 = (s32[4,1024]{1,0:T(4,128)S(1)}, s32[4,1024]{1,0:T(4,128)S(1)}, u32[]{:S(2)}, u32[]{:S(2)}) collective-permute-start(s32[4,1024]{1,0:T(4,128)S(1)} %add_select_fusion.2), channel_id=1, source_target_pairs={{0,4},{1,5},{2,6},{3,7},{4,0},{5,1},{6,2},{7,3},{8,12},{9,13},{10,... | collective-permute-start | bytes 49160 | tf_op jit(solution)/shard_map/ppermute | solution.py:36
  26.2 3.3 %stack.13.ends = s32[5]{0:T(128)S(1)} concatenate(s32[1]{0:T(128)} %get-tuple-element.190, s32[1]{0:T(128)} %get-tuple-element.189, s32[1]{0:T(128)} %get-tuple-element.188, s32[1]{0:T(128)} %get-tuple-element.187, s32[1]{0:T(128)} %bitcast.4), dimensions={0} | concatenate | bytes 40 | tf_op jit(solution)/shard_map/stack | solution.py:269
  33.2 2.7 %collective-permute-start.5 = (bf16[1024,256]{1,0:T(8,128)(2,1)S(1)}, bf16[1024,256]{1,0:T(8,128)(2,1)S(1)}, u32[]{:S(2)}, u32[]{:S(2)}) collective-permute-start(bf16[1024,256]{1,0:T(8,128)(2,1)S(1)} %bitcast.35), channel_id=1, source_target_pairs={{0,48},{1,49},{2,50},{3,51},{4,52},{5,53},{6,54},{7,55},{8,56},{9,... | collective-permute-start | bytes 1572872 | tf_op jit(solution)/shard_map/ppermute | solution.py:31
  35.9 7.4 %shard_map.120 = (bf16[32,8192]{1,0:T(8,128)(2,1)S(1)}, bf16[320,128,128]{2,1,0:T(8,128)(2,1)S(1)}) custom-call(s32[320]{0:T(512)S(1)} %get-tuple-element.151.src, s32[320]{0:T(512)S(1)} %get-tuple-element.184.dst, s32[1]{0:T(128)} %bitcast.31.live, bf16[320,128,128]{2,1,0:T(8,128)(2,1)} %bitcast.38, s32[128,1,128]{2,1,0:T(1,128)S(1)} %select_n.380.ids), custom_call_target="tpu_custom_call" | custom-call | flops 167772160 | bytes 10485760 | tf_op jit(solution)/shard_map/pallas_call | solution.py:127
  44.4 8.8 %collective-permute-done.6.refs_3_ = bf16[1024,256]{1,0:T(8,128)(2,1)S(1)} collective-permute-done((bf16[1024,256]{1,0:T(8,128)(2,1)S(1)}, bf16[1024,256]{1,0:T(8,128)(2,1)S(1)}, u32[]{:S(2)}, u32[]{:S(2)}) %collective-permute-start.6) | collective-permute-done | bytes 524320 | tf_op jit(solution)/shard_map/ppermute | solution.py:31
  54.1 6.3 %shard_map.122 = bf16[8192,256]{1,0:T(8,128)(2,1)S(1)} custom-call(s32[288]{0:T(512)S(1)} %get-tuple-element.137.c0, s32[288]{0:T(512)S(1)} %get-tuple-element.136.c1, s32[288]{0:T(512)S(1)} %multiply_add_fusion.to, s32[5]{0:T(128)S(1)} %stack.13.ends, bf16[320,128,128]{2,1,0:T(8,128)(2,1)S(1)} %get-tuple-element.72.adj, ...), custom_call_target="tpu_custom_call" | custom-call | flops 1342177280 | bytes 5242880 | tf_op jit(solution)/shard_map/pallas_call | solution.py:127
  66.6 3.1 %shard_map.123 = bf16[4096,256]{1,0:T(8,128)(2,1)S(1)} custom-call(s32[288]{0:T(512)S(1)} %get-tuple-element.137.c0, s32[288]{0:T(512)S(1)} %get-tuple-element.136.c1, s32[288]{0:T(512)S(1)} %multiply_add_fusion.to, s32[5]{0:T(128)S(1)} %stack.13.ends, bf16[320,128,128]{2,1,0:T(8,128)(2,1)S(1)} %get-tuple-element.72.adj, ...), custom_call_target="tpu_custom_call" | custom-call | flops 1342177280 | bytes 5242880 | tf_op jit(solution)/shard_map/pallas_call | solution.py:127
  73.8 3.3 %shard_map.124 = bf16[4096,256]{1,0:T(8,128)(2,1)S(1)} custom-call(s32[288]{0:T(512)S(1)} %get-tuple-element.137.c0, s32[288]{0:T(512)S(1)} %get-tuple-element.136.c1, s32[288]{0:T(512)S(1)} %multiply_add_fusion.to, s32[5]{0:T(128)S(1)} %stack.13.ends, bf16[320,128,128]{2,1,0:T(8,128)(2,1)S(1)} %get-tuple-element.72.adj, ...), custom_call_target="tpu_custom_call" | custom-call | flops 1342177280 | bytes 5242880 | tf_op jit(solution)/shard_map/pallas_call | solution.py:127
  77.1 3.9 %collective-permute-start.15 = (f32[16,256]{1,0:T(8,128)S(1)}, f32[16,256]{1,0:T(8,128)S(1)}, u32[]{:S(2)}, u32[]{:S(2)}) collective-permute-start(f32[16,256]{1,0:T(8,128)S(1)} %add.500), channel_id=1, source_target_pairs={{0,32},{1,33},{2,34},{3,35},{4,36},{5,37},{6,38},{7,39},{8,40},{9,... | collective-permute-start | bytes 49160 | tf_op jit(solution)/shard_map/ppermute | solution.py:36
  82.2 4.3 %collective-permute-start.16 = (f32[16,256]{1,0:T(8,128)S(1)}, f32[16,256]{1,0:T(8,128)S(1)}, u32[]{:S(2)}, u32[]{:S(2)}) collective-permute-start(f32[16,256]{1,0:T(8,128)S(1)} %add.501), channel_id=1, source_target_pairs={{0,1},{1,0},{2,3},{3,2},{4,5},{5,4},{6,7},{7,6},{8,9},{9,8},{10,11... | collective-permute-start | bytes 49160 | tf_op jit(solution)/shard_map/ppermute | solution.py:36
  94.9 10.4 %collective-permute-done.22.refs_3_ = bf16[1056,256]{1,0:T(8,128)(2,1)S(1)} collective-permute-done((bf16[1056,256]{1,0:T(8,128)(2,1)}, bf16[1056,256]{1,0:T(8,128)(2,1)S(1)}, u32[]{:S(2)}, u32[]{:S(2)}) %collective-permute-start.22) | collective-permute-done | bytes 540704 | tf_op jit(solution)/shard_map/ppermute | solution.py:31
  106.5 11.9 %collective-permute-done.20.refs_1_ = bf16[1056,256]{1,0:T(8,128)(2,1)S(1)} collective-permute-done((bf16[1056,256]{1,0:T(8,128)(2,1)}, bf16[1056,256]{1,0:T(8,128)(2,1)S(1)}, u32[]{:S(2)}, u32[]{:S(2)}) %collective-permute-start.20) | collective-permute-done | bytes 540704 | tf_op jit(solution)/shard_map/ppermute | solution.py:31
  119.3 3.9 %shard_map.125 = (bf16[1024,256]{1,0:T(8,128)(2,1)S(1)}, bf16[1024,512]{1,0:T(8,128)(2,1)S(1)}, bf16[1024,512]{1,0:T(8,128)(2,1)S(1)}, bf16[1024,256]{1,0:T(8,128)(2,1)S(1)}, bf16[32,256]{1,0:T(8,128)(2,1)S(1)}) custom-call(s32[1,1024]{1,0:T(1,128)S(1)} %copy-done.5, f32[16,256]{1,0:T(8,128)S(1)} %fusion.14.pooled, bf16[256,512]{1,0:T(8,128)(2,1)S(1)} %copy-done.4, ...), custom_call_target="tpu_custom_call" | custom-call | flops 805306368 | bytes 2097152 | tf_op jit(solution)/shard_map/pallas_call | solution.py:127
  123.2 2.7 %collective-permute-start.30 = (bf16[1024,256]{1,0:T(8,128)(2,1)S(1)}, bf16[1024,256]{1,0:T(8,128)(2,1)S(1)}, u32[]{:S(2)}, u32[]{:S(2)}) collective-permute-start(bf16[1024,256]{1,0:T(8,128)(2,1)S(1)} %get-tuple-element.90.refs_0_), channel_id=1, source_target_pairs={{0,6},{1,7},{2,0},{3,1},{4,2},{5,3},{6,4},{7,5},{8,14},{9,15},{10,... | collective-permute-start | bytes 1572872 | tf_op jit(solution)/shard_map/ppermute | solution.py:31
  130.0 8.5 %collective-permute-done.26.refs_4_ = bf16[1024,256]{1,0:T(8,128)(2,1)S(1)} collective-permute-done((bf16[1024,256]{1,0:T(8,128)(2,1)S(1)}, bf16[1024,256]{1,0:T(8,128)(2,1)S(1)}, u32[]{:S(2)}, u32[]{:S(2)}) %collective-permute-start.26) | collective-permute-done | bytes 524320 | tf_op jit(solution)/shard_map/ppermute | solution.py:31
  138.5 7.6 %collective-permute-done.25.refs_2_ = bf16[1024,256]{1,0:T(8,128)(2,1)S(1)} collective-permute-done((bf16[1024,256]{1,0:T(8,128)(2,1)S(1)}, bf16[1024,256]{1,0:T(8,128)(2,1)S(1)}, u32[]{:S(2)}, u32[]{:S(2)}) %collective-permute-start.25) | collective-permute-done | bytes 524320 | tf_op jit(solution)/shard_map/ppermute | solution.py:31
  150.2 2.8 %collective-permute-start.27 = (bf16[1312,256]{1,0:T(8,128)(2,1)S(1)}, bf16[1312,256]{1,0:T(8,128)(2,1)S(1)}, u32[]{:S(2)}, u32[]{:S(2)}) collective-permute-start(bf16[1312,256]{1,0:T(8,128)(2,1)S(1)} %get-tuple-element.164), channel_id=1, source_target_pairs={{0,6},{1,7},{2,0},{3,1},{4,2},{5,3},{6,4},{7,5},{8,14},{9,15},{10,... | collective-permute-start | bytes 2015240 | tf_op jit(solution)/shard_map/ppermute | solution.py:31
  156.2 16.6 %collective-permute-done.24 = bf16[288,256]{1,0:T(8,128)(2,1)S(1)} collective-permute-done((bf16[288,256]{1,0:T(8,128)(2,1)S(1)}, bf16[288,256]{1,0:T(8,128)(2,1)S(1)}, u32[]{:S(2)}, u32[]{:S(2)}) %collective-permute-start.24) | collective-permute-done | bytes 147488 | tf_op jit(solution)/shard_map/ppermute | solution.py:31
  177.5 2.9 %collective-permute-done.29 = bf16[288,256]{1,0:T(8,128)(2,1)S(1)} collective-permute-done((bf16[288,256]{1,0:T(8,128)(2,1)S(1)}, bf16[288,256]{1,0:T(8,128)(2,1)S(1)}, u32[]{:S(2)}, u32[]{:S(2)}) %collective-permute-start.29) | collective-permute-done | bytes 147488 | tf_op jit(solution)/shard_map/ppermute | solution.py:36
  180.5 4.1 %shard_map.126 = (bf16[16512,256]{1,0:T(8,128)(2,1)S(1)}, bf16[320,128,128]{2,1,0:T(8,128)(2,1)S(1)}) custom-call(bf16[320,128,128]{2,1,0:T(8,128)(2,1)} %bitcast.39, bf16[1024,256]{1,0:T(8,128)(2,1)S(1)} %get-tuple-element.90.refs_0_, bf16[1024,256]{1,0:T(8,128)(2,1)S(1)} %collective-permute-done.30.refs_1_, ...), custom_call_target="tpu_custom_call" | custom-call | bytes 10485760 | tf_op jit(solution)/shard_map/pallas_call | solution.py:127
  187.2 5.4 %shard_map.127 = (bf16[1088,256]{1,0:T(8,128)(2,1)S(1)}, bf16[1088,256]{1,0:T(8,128)(2,1)S(1)}, bf16[1088,256]{1,0:T(8,128)(2,1)S(1)}, bf16[1088,256]{1,0:T(8,128)(2,1)S(1)}) custom-call(s32[224]{0:T(256)S(1)} %get-tuple-element.139.c0, s32[224]{0:T(256)S(1)} %get-tuple-element.138.c1, s32[224]{0:T(256)S(1)} %multiply_add_fusion.1.to, ...), custom_call_target="tpu_custom_call" | custom-call | flops 1342177280 | bytes 5242880 | tf_op jit(solution)/shard_map/pallas_call | solution.py:127
  197.1 3.3 %collective-permute-start.41 = (bf16[1088,256]{1,0:T(8,128)(2,1)S(1)}, bf16[1088,256]{1,0:T(8,128)(2,1)S(1)}, u32[]{:S(2)}, u32[]{:S(2)}) collective-permute-start(bf16[1088,256]{1,0:T(8,128)(2,1)S(1)} %get-tuple-element.110), channel_id=1, source_target_pairs={{0,64},{1,65},{2,66},{3,67},{4,68},{5,69},{6,70},{7,71},{8,72},{9,... | collective-permute-start | bytes 1671176 | tf_op jit(solution)/shard_map/ppermute | solution.py:31
  200.4 5.1 %shard_map.128 = (bf16[1088,256]{1,0:T(8,128)(2,1)S(1)}, bf16[1088,256]{1,0:T(8,128)(2,1)S(1)}, bf16[1088,256]{1,0:T(8,128)(2,1)S(1)}, bf16[1088,256]{1,0:T(8,128)(2,1)S(1)}) custom-call(s32[224]{0:T(256)S(1)} %get-tuple-element.139.c0, s32[224]{0:T(256)S(1)} %get-tuple-element.138.c1, s32[224]{0:T(256)S(1)} %multiply_add_fusion.1.to, ...), custom_call_target="tpu_custom_call" | custom-call | flops 1342177280 | bytes 5242880 | tf_op jit(solution)/shard_map/pallas_call | solution.py:127
  205.6 5.2 %collective-permute-done.39 = bf16[1088,256]{1,0:T(8,128)(2,1)S(1)} collective-permute-done((bf16[1088,256]{1,0:T(8,128)(2,1)S(1)}, bf16[1088,256]{1,0:T(8,128)(2,1)S(1)}, u32[]{:S(2)}, u32[]{:S(2)}) %collective-permute-start.39) | collective-permute-done | bytes 557088 | tf_op jit(solution)/shard_map/ppermute | solution.py:31
  211.2 3.3 %collective-permute-start.42 = (bf16[288,256]{1,0:T(8,128)(2,1)S(1)}, bf16[288,256]{1,0:T(8,128)(2,1)S(1)}, u32[]{:S(2)}, u32[]{:S(2)}) collective-permute-start(bf16[288,256]{1,0:T(8,128)(2,1)S(1)} %pad_maximum_fusion.16), channel_id=1, source_target_pairs={{0,1},{1,0},{2,3},{3,2},{4,5},{5,4},{6,7},{7,6},{8,9},{9,8},{10,11... | collective-permute-start | bytes 442376 | tf_op jit(solution)/shard_map/ppermute | solution.py:36
  214.4 3.0 %collective-permute-start.47 = (bf16[1088,256]{1,0:T(8,128)(2,1)S(1)}, bf16[1088,256]{1,0:T(8,128)(2,1)S(1)}, u32[]{:S(2)}, u32[]{:S(2)}) collective-permute-start(bf16[1088,256]{1,0:T(8,128)(2,1)S(1)} %add_convert_fusion.1), channel_id=1, source_target_pairs={{0,64},{1,65},{2,66},{3,67},{4,68},{5,69},{6,70},{7,71},{8,72},{9,... | collective-permute-start | bytes 1671176 | tf_op jit(solution)/shard_map/ppermute | solution.py:31
  220.9 13.0 %collective-permute-done.43 = bf16[288,256]{1,0:T(8,128)(2,1)S(1)} collective-permute-done((bf16[288,256]{1,0:T(8,128)(2,1)S(1)}, bf16[288,256]{1,0:T(8,128)(2,1)S(1)}, u32[]{:S(2)}, u32[]{:S(2)}) %collective-permute-start.43) | collective-permute-done | bytes 147488 | tf_op jit(solution)/shard_map/ppermute | solution.py:36
  234.1 4.1 %collective-permute-done.48 = bf16[256,256]{1,0:T(8,128)(2,1)S(1)} collective-permute-done((bf16[256,256]{1,0:T(8,128)(2,1)S(1)}, bf16[256,256]{1,0:T(8,128)(2,1)S(1)}, u32[]{:S(2)}, u32[]{:S(2)}) %collective-permute-start.48) | collective-permute-done | bytes 131104 | tf_op jit(solution)/shard_map/ppermute | solution.py:36
  239.0 6.6 %collective-permute-done.44.refs_1_ = bf16[1088,256]{1,0:T(8,128)(2,1)S(1)} collective-permute-done((bf16[1088,256]{1,0:T(8,128)(2,1)S(1)}, bf16[1088,256]{1,0:T(8,128)(2,1)S(1)}, u32[]{:S(2)}, u32[]{:S(2)}) %collective-permute-start.44) | collective-permute-done | bytes 557088 | tf_op jit(solution)/shard_map/ppermute | solution.py:31
  247.3 3.2 %shard_map.129 = f32[1024,256]{1,0:T(8,128)} custom-call(f32[16,256]{1,0:T(8,128)} %fusion.15.gp, bf16[1088,256]{1,0:T(8,128)(2,1)} %copy-done.1, bf16[1088,256]{1,0:T(8,128)(2,1)} %copy-done.8, bf16[1088,256]{1,0:T(8,128)(2,1)} %copy-done.7, bf16[1088,256]{1,0:T(8,128)(2,1)} %copy-done.9, bf16[1088,256]{1,0:T(8,128)(2,1)} %copy-done.6), custom_call_target="tpu_custom_call" | custom-call | tf_op jit(solution)/shard_map/pallas_call | solution.py:418
  (191 shorter events, 73.7 us)
Async XLA Ops:
  0.6 28.9 %collective-permute-start.7 = (bf16[1024,256]{1,0:T(8,128)(2,1)}, bf16[1024,256]{1,0:T(8,128)(2,1)S(1)}, u32[]{:S(2)}, u32[]{:S(2)}) collective-permute-start(bf16[1024,256]{1,0:T(8,128)(2,1)} %bitcast.32), channel_id=1, source_target_pairs={{0,64},{1,65},{2,66},{3,67},{4,68},{5,69},{6,70},{7,71},{8,72},{9,... | collective-permute-start | bytes 1572872 | tf_op jit(solution)/shard_map/ppermute | solution.py:31
  5.1 24.4 %collective-permute-start = (bf16[1024,256]{1,0:T(8,128)(2,1)}, bf16[1024,256]{1,0:T(8,128)(2,1)S(1)}, u32[]{:S(2)}, u32[]{:S(2)}) collective-permute-start(bf16[1024,256]{1,0:T(8,128)(2,1)} %bitcast.33), channel_id=1, source_target_pairs={{0,32},{1,33},{2,34},{3,35},{4,36},{5,37},{6,38},{7,39},{8,40},{9,... | collective-permute-start | bytes 1572872 | tf_op jit(solution)/shard_map/ppermute | solution.py:31
  29.6 13.7 %collective-permute-start.10 = (bf16[1024,256]{1,0:T(8,128)(2,1)S(1)}, bf16[1024,256]{1,0:T(8,128)(2,1)S(1)}, u32[]{:S(2)}, u32[]{:S(2)}) collective-permute-start(bf16[1024,256]{1,0:T(8,128)(2,1)S(1)} %collective-permute-done.7.refs_4_), channel_id=1, source_target_pairs={{0,16},{1,17},{2,18},{3,19},{4,20},{5,21},{6,22},{7,23},{8,24},{9,... | collective-permute-start | bytes 1572872 | tf_op jit(solution)/shard_map/ppermute | solution.py:31
  30.1 13.3 %collective-permute-start.8 = (bf16[1024,256]{1,0:T(8,128)(2,1)S(1)}, bf16[1024,256]{1,0:T(8,128)(2,1)S(1)}, u32[]{:S(2)}, u32[]{:S(2)}) collective-permute-start(bf16[1024,256]{1,0:T(8,128)(2,1)S(1)} %collective-permute-done.7.refs_4_), channel_id=1, source_target_pairs={{0,48},{1,49},{2,50},{3,51},{4,52},{5,53},{6,54},{7,55},{8,56},{9,... | collective-permute-start | bytes 1572872 | tf_op jit(solution)/shard_map/ppermute | solution.py:31
  33.2 20.0 %collective-permute-start.6 = (bf16[1024,256]{1,0:T(8,128)(2,1)S(1)}, bf16[1024,256]{1,0:T(8,128)(2,1)S(1)}, u32[]{:S(2)}, u32[]{:S(2)}) collective-permute-start(bf16[1024,256]{1,0:T(8,128)(2,1)S(1)} %bitcast.34), channel_id=1, source_target_pairs={{0,16},{1,17},{2,18},{3,19},{4,20},{5,21},{6,22},{7,23},{8,24},{9,... | collective-permute-start | bytes 1572872 | tf_op jit(solution)/shard_map/ppermute | solution.py:31
  33.2 20.0 %collective-permute-start.5 = (bf16[1024,256]{1,0:T(8,128)(2,1)S(1)}, bf16[1024,256]{1,0:T(8,128)(2,1)S(1)}, u32[]{:S(2)}, u32[]{:S(2)}) collective-permute-start(bf16[1024,256]{1,0:T(8,128)(2,1)S(1)} %bitcast.35), channel_id=1, source_target_pairs={{0,48},{1,49},{2,50},{3,51},{4,52},{5,53},{6,54},{7,55},{8,56},{9,... | collective-permute-start | bytes 1572872 | tf_op jit(solution)/shard_map/ppermute | solution.py:31
  70.3 17.0 %collective-permute-start.18 = (bf16[1024,256]{1,0:T(8,128)(2,1)S(1)}, bf16[1024,256]{1,0:T(8,128)(2,1)S(1)}, u32[]{:S(2)}, u32[]{:S(2)}) collective-permute-start(bf16[1024,256]{1,0:T(8,128)(2,1)S(1)} %get-tuple-element.160), channel_id=1, source_target_pairs={{0,6},{1,7},{2,0},{3,1},{4,2},{5,3},{6,4},{7,5},{8,14},{9,15},{10,... | collective-permute-start | bytes 1572872 | tf_op jit(solution)/shard_map/ppermute | solution.py:31
  72.6 14.7 %collective-permute-start.19 = (bf16[1024,256]{1,0:T(8,128)(2,1)S(1)}, bf16[1024,256]{1,0:T(8,128)(2,1)S(1)}, u32[]{:S(2)}, u32[]{:S(2)}) collective-permute-start(bf16[1024,256]{1,0:T(8,128)(2,1)S(1)} %get-tuple-element.161), channel_id=1, source_target_pairs={{0,8},{1,9},{2,10},{3,11},{4,12},{5,13},{6,14},{7,15},{8,0},{9,1},... | collective-permute-start | bytes 1572872 | tf_op jit(solution)/shard_map/ppermute | solution.py:31
  73.8 13.5 %collective-permute-start.17 = (bf16[1024,256]{1,0:T(8,128)(2,1)S(1)}, bf16[1024,256]{1,0:T(8,128)(2,1)S(1)}, u32[]{:S(2)}, u32[]{:S(2)}) collective-permute-start(bf16[1024,256]{1,0:T(8,128)(2,1)S(1)} %get-tuple-element.162), channel_id=1, source_target_pairs={{0,2},{1,3},{2,4},{3,5},{4,6},{5,7},{6,0},{7,1},{8,10},{9,11},{10,... | collective-permute-start | bytes 1572872 | tf_op jit(solution)/shard_map/ppermute | solution.py:31
  89.1 16.2 %collective-permute-start.22 = (bf16[1056,256]{1,0:T(8,128)(2,1)}, bf16[1056,256]{1,0:T(8,128)(2,1)S(1)}, u32[]{:S(2)}, u32[]{:S(2)}) collective-permute-start(bf16[1056,256]{1,0:T(8,128)(2,1)} %get-tuple-element.179), channel_id=1, source_target_pairs={{0,6},{1,7},{2,0},{3,1},{4,2},{5,3},{6,4},{7,5},{8,14},{9,15},{10,... | collective-permute-start | bytes 1622024 | tf_op jit(solution)/shard_map/ppermute | solution.py:31
  91.5 15.0 %collective-permute-start.21 = (bf16[1056,256]{1,0:T(8,128)(2,1)}, bf16[1056,256]{1,0:T(8,128)(2,1)S(1)}, u32[]{:S(2)}, u32[]{:S(2)}) collective-permute-start(bf16[1056,256]{1,0:T(8,128)(2,1)} %get-tuple-element.180), channel_id=1, source_target_pairs={{0,4},{1,5},{2,6},{3,7},{4,0},{5,1},{6,2},{7,3},{8,12},{9,13},{10,... | collective-permute-start | bytes 1622024 | tf_op jit(solution)/shard_map/ppermute | solution.py:31
  91.5 26.8 %collective-permute-start.20 = (bf16[1056,256]{1,0:T(8,128)(2,1)}, bf16[1056,256]{1,0:T(8,128)(2,1)S(1)}, u32[]{:S(2)}, u32[]{:S(2)}) collective-permute-start(bf16[1056,256]{1,0:T(8,128)(2,1)} %get-tuple-element.181), channel_id=1, source_target_pairs={{0,2},{1,3},{2,4},{3,5},{4,6},{5,7},{6,0},{7,1},{8,10},{9,11},{10,... | collective-permute-start | bytes 1622024 | tf_op jit(solution)/shard_map/ppermute | solution.py:31
  93.2 25.2 %collective-permute-start.23 = (bf16[1024,256]{1,0:T(8,128)(2,1)}, bf16[1024,256]{1,0:T(8,128)(2,1)}, u32[]{:S(2)}, u32[]{:S(2)}) collective-permute-start(bf16[1024,256]{1,0:T(8,128)(2,1)} %add_convert_fusion.2), channel_id=1, source_target_pairs={{0,8},{1,9},{2,10},{3,11},{4,12},{5,13},{6,14},{7,15},{8,0},{9,1},... | collective-permute-start | bytes 1572872 | tf_op jit(solution)/shard_map/ppermute | solution.py:31
  123.2 25.1 %collective-permute-start.31 = (bf16[1024,256]{1,0:T(8,128)(2,1)S(1)}, bf16[1024,256]{1,0:T(8,128)(2,1)S(1)}, u32[]{:S(2)}, u32[]{:S(2)}) collective-permute-start(bf16[1024,256]{1,0:T(8,128)(2,1)S(1)} %get-tuple-element.90.refs_0_), channel_id=1, source_target_pairs={{0,2},{1,3},{2,4},{3,5},{4,6},{5,7},{6,0},{7,1},{8,10},{9,11},{10,... | collective-permute-start | bytes 1572872 | tf_op jit(solution)/shard_map/ppermute | solution.py:31
  123.2 23.0 %collective-permute-start.30 = (bf16[1024,256]{1,0:T(8,128)(2,1)S(1)}, bf16[1024,256]{1,0:T(8,128)(2,1)S(1)}, u32[]{:S(2)}, u32[]{:S(2)}) collective-permute-start(bf16[1024,256]{1,0:T(8,128)(2,1)S(1)} %get-tuple-element.90.refs_0_), channel_id=1, source_target_pairs={{0,6},{1,7},{2,0},{3,1},{4,2},{5,3},{6,4},{7,5},{8,14},{9,15},{10,... | collective-permute-start | bytes 1572872 | tf_op jit(solution)/shard_map/ppermute | solution.py:31
  125.9 12.7 %collective-permute-start.26 = (bf16[1024,256]{1,0:T(8,128)(2,1)S(1)}, bf16[1024,256]{1,0:T(8,128)(2,1)S(1)}, u32[]{:S(2)}, u32[]{:S(2)}) collective-permute-start(bf16[1024,256]{1,0:T(8,128)(2,1)S(1)} %get-tuple-element.90.refs_0_), channel_id=1, source_target_pairs={{0,8},{1,9},{2,10},{3,11},{4,12},{5,13},{6,14},{7,15},{8,0},{9,1},... | collective-permute-start | bytes 1572872 | tf_op jit(solution)/shard_map/ppermute | solution.py:31
  127.7 18.5 %collective-permute-start.25 = (bf16[1024,256]{1,0:T(8,128)(2,1)S(1)}, bf16[1024,256]{1,0:T(8,128)(2,1)S(1)}, u32[]{:S(2)}, u32[]{:S(2)}) collective-permute-start(bf16[1024,256]{1,0:T(8,128)(2,1)S(1)} %get-tuple-element.90.refs_0_), channel_id=1, source_target_pairs={{0,4},{1,5},{2,6},{3,7},{4,0},{5,1},{6,2},{7,3},{8,12},{9,13},{10,... | collective-permute-start | bytes 1572872 | tf_op jit(solution)/shard_map/ppermute | solution.py:31
  148.3 32.1 %collective-permute-start.33 = (bf16[5120,256]{1,0:T(8,128)(2,1)S(1)}, bf16[5120,256]{1,0:T(8,128)(2,1)S(1)}, u32[]{:S(2)}, u32[]{:S(2)}) collective-permute-start(bf16[5120,256]{1,0:T(8,128)(2,1)S(1)} %constant_dynamic-update-slice_fusion), channel_id=1, source_target_pairs={{0,1},{1,0},{2,3},{3,2},{4,5},{5,4},{6,7},{7,6},{8,9},{9,8},{10,11... | collective-permute-start | bytes 7864328 | tf_op jit(solution)/shard_map/ppermute | solution.py:31
  150.2 22.6 %collective-permute-start.27 = (bf16[1312,256]{1,0:T(8,128)(2,1)S(1)}, bf16[1312,256]{1,0:T(8,128)(2,1)S(1)}, u32[]{:S(2)}, u32[]{:S(2)}) collective-permute-start(bf16[1312,256]{1,0:T(8,128)(2,1)S(1)} %get-tuple-element.164), channel_id=1, source_target_pairs={{0,6},{1,7},{2,0},{3,1},{4,2},{5,3},{6,4},{7,5},{8,14},{9,15},{10,... | collective-permute-start | bytes 2015240 | tf_op jit(solution)/shard_map/ppermute | solution.py:31
  153.1 20.8 %collective-permute-start.28 = (bf16[1312,256]{1,0:T(8,128)(2,1)S(1)}, bf16[1312,256]{1,0:T(8,128)(2,1)S(1)}, u32[]{:S(2)}, u32[]{:S(2)}) collective-permute-start(bf16[1312,256]{1,0:T(8,128)(2,1)S(1)} %get-tuple-element.165), channel_id=1, source_target_pairs={{0,2},{1,3},{2,4},{3,5},{4,6},{5,7},{6,0},{7,1},{8,10},{9,11},{10,... | collective-permute-start | bytes 2015240 | tf_op jit(solution)/shard_map/ppermute | solution.py:31
  153.1 19.7 %collective-permute-start.24 = (bf16[288,256]{1,0:T(8,128)(2,1)S(1)}, bf16[288,256]{1,0:T(8,128)(2,1)S(1)}, u32[]{:S(2)}, u32[]{:S(2)}) collective-permute-start(bf16[288,256]{1,0:T(8,128)(2,1)S(1)} %pad_maximum_fusion.11), channel_id=1, source_target_pairs={{0,4},{1,5},{2,6},{3,7},{4,0},{5,1},{6,2},{7,3},{8,12},{9,13},{10,... | collective-permute-start | bytes 442376 | tf_op jit(solution)/shard_map/ppermute | solution.py:31
  154.5 22.3 %collective-permute-start.32 = (bf16[1024,256]{1,0:T(8,128)(2,1)S(1)}, bf16[1024,256]{1,0:T(8,128)(2,1)S(1)}, u32[]{:S(2)}, u32[]{:S(2)}) collective-permute-start(bf16[1024,256]{1,0:T(8,128)(2,1)S(1)} %collective-permute-done.25.refs_2_), channel_id=1, source_target_pairs={{0,8},{1,9},{2,10},{3,11},{4,12},{5,13},{6,14},{7,15},{8,0},{9,1},... | collective-permute-start | bytes 1572872 | tf_op jit(solution)/shard_map/ppermute | solution.py:31
  192.7 12.8 %collective-permute-start.38 = (bf16[288,256]{1,0:T(8,128)(2,1)S(1)}, bf16[288,256]{1,0:T(8,128)(2,1)S(1)}, u32[]{:S(2)}, u32[]{:S(2)}) collective-permute-start(bf16[288,256]{1,0:T(8,128)(2,1)S(1)} %pad_maximum_fusion.15), channel_id=1, source_target_pairs={{0,32},{1,33},{2,34},{3,35},{4,36},{5,37},{6,38},{7,39},{8,40},{9,... | collective-permute-start | bytes 442376 | tf_op jit(solution)/shard_map/ppermute | solution.py:36
  194.4 16.3 %collective-permute-start.39 = (bf16[1088,256]{1,0:T(8,128)(2,1)S(1)}, bf16[1088,256]{1,0:T(8,128)(2,1)S(1)}, u32[]{:S(2)}, u32[]{:S(2)}) collective-permute-start(bf16[1088,256]{1,0:T(8,128)(2,1)S(1)} %get-tuple-element.108), channel_id=1, source_target_pairs={{0,16},{1,17},{2,18},{3,19},{4,20},{5,21},{6,22},{7,23},{8,24},{9,... | collective-permute-start | bytes 1671176 | tf_op jit(solution)/shard_map/ppermute | solution.py:31
  196.1 14.7 %collective-permute-start.40 = (bf16[1088,256]{1,0:T(8,128)(2,1)S(1)}, bf16[1088,256]{1,0:T(8,128)(2,1)S(1)}, u32[]{:S(2)}, u32[]{:S(2)}) collective-permute-start(bf16[1088,256]{1,0:T(8,128)(2,1)S(1)} %get-tuple-element.109), channel_id=1, source_target_pairs={{0,48},{1,49},{2,50},{3,51},{4,52},{5,53},{6,54},{7,55},{8,56},{9,... | collective-permute-start | bytes 1671176 | tf_op jit(solution)/shard_map/ppermute | solution.py:31
  197.1 13.6 %collective-permute-start.41 = (bf16[1088,256]{1,0:T(8,128)(2,1)S(1)}, bf16[1088,256]{1,0:T(8,128)(2,1)S(1)}, u32[]{:S(2)}, u32[]{:S(2)}) collective-permute-start(bf16[1088,256]{1,0:T(8,128)(2,1)S(1)} %get-tuple-element.110), channel_id=1, source_target_pairs={{0,64},{1,65},{2,66},{3,67},{4,68},{5,69},{6,70},{7,71},{8,72},{9,... | collective-permute-start | bytes 1671176 | tf_op jit(solution)/shard_map/ppermute | solution.py:31
  214.4 19.5 %collective-permute-start.47 = (bf16[1088,256]{1,0:T(8,128)(2,1)S(1)}, bf16[1088,256]{1,0:T(8,128)(2,1)S(1)}, u32[]{:S(2)}, u32[]{:S(2)}) collective-permute-start(bf16[1088,256]{1,0:T(8,128)(2,1)S(1)} %add_convert_fusion.1), channel_id=1, source_target_pairs={{0,64},{1,65},{2,66},{3,67},{4,68},{5,69},{6,70},{7,71},{8,72},{9,... | collective-permute-start | bytes 1671176 | tf_op jit(solution)/shard_map/ppermute | solution.py:31
  217.5 16.4 %collective-permute-start.43 = (bf16[288,256]{1,0:T(8,128)(2,1)S(1)}, bf16[288,256]{1,0:T(8,128)(2,1)S(1)}, u32[]{:S(2)}, u32[]{:S(2)}) collective-permute-start(bf16[288,256]{1,0:T(8,128)(2,1)S(1)} %pad_maximum_fusion.17), channel_id=1, source_target_pairs={{0,8},{1,9},{2,10},{3,11},{4,12},{5,13},{6,14},{7,15},{8,0},{9,1},... | collective-permute-start | bytes 442376 | tf_op jit(solution)/shard_map/ppermute | solution.py:36
  218.2 20.8 %collective-permute-start.45 = (bf16[1088,256]{1,0:T(8,128)(2,1)S(1)}, bf16[1088,256]{1,0:T(8,128)(2,1)S(1)}, u32[]{:S(2)}, u32[]{:S(2)}) collective-permute-start(bf16[1088,256]{1,0:T(8,128)(2,1)S(1)} %add_convert_fusion), channel_id=1, source_target_pairs={{0,32},{1,33},{2,34},{3,35},{4,36},{5,37},{6,38},{7,39},{8,40},{9,... | collective-permute-start | bytes 1671176 | tf_op jit(solution)/shard_map/ppermute | solution.py:31
  218.3 27.4 %collective-permute-start.44 = (bf16[1088,256]{1,0:T(8,128)(2,1)S(1)}, bf16[1088,256]{1,0:T(8,128)(2,1)S(1)}, u32[]{:S(2)}, u32[]{:S(2)}) collective-permute-start(bf16[1088,256]{1,0:T(8,128)(2,1)S(1)} %get-tuple-element.121), channel_id=1, source_target_pairs={{0,16},{1,17},{2,18},{3,19},{4,20},{5,21},{6,22},{7,23},{8,24},{9,... | collective-permute-start | bytes 1671176 | tf_op jit(solution)/shard_map/ppermute | solution.py:31
  219.4 26.2 %collective-permute-start.46 = (bf16[1088,256]{1,0:T(8,128)(2,1)S(1)}, bf16[1088,256]{1,0:T(8,128)(2,1)S(1)}, u32[]{:S(2)}, u32[]{:S(2)}) collective-permute-start(bf16[1088,256]{1,0:T(8,128)(2,1)S(1)} %get-tuple-element.122), channel_id=1, source_target_pairs={{0,48},{1,49},{2,50},{3,51},{4,52},{5,53},{6,54},{7,55},{8,56},{9,... | collective-permute-start | bytes 1671176 | tf_op jit(solution)/shard_map/ppermute | solution.py:31
  238.3 12.2 %collective-permute-start.49 = (bf16[512,256]{1,0:T(8,128)(2,1)S(1)}, bf16[512,256]{1,0:T(8,128)(2,1)S(1)}, u32[]{:S(2)}, u32[]{:S(2)}) collective-permute-start(bf16[512,256]{1,0:T(8,128)(2,1)S(1)} %maximum_select_fusion.1), channel_id=1, source_target_pairs={{0,4},{1,5},{2,6},{3,7},{4,0},{5,1},{6,2},{7,3},{8,12},{9,13},{10,... | collective-permute-start | bytes 786440 | tf_op jit(solution)/shard_map/ppermute | solution.py:36
  (28 other events, 248.7 us)

commit v2 on v1

--- a/solution.py
+++ b/solution.py
@@ -97,11 +97,18 @@
     return take(place), take(1 - place).astype(BF16)
 
 
-def agree(weights, pool, *step):
-    terms = jnp.concatenate([weights.astype(BF16), *split(pool)])
-    total = terms.astype(F32) + swap(terms, *step).astype(F32)
-    n = weights.shape[0]
+def as_sent(weights, pool):
+    return jnp.concatenate([weights.astype(BF16), *split(pool)])
+
+
+def as_held(total):
+    n = total.shape[0] - 2 * VN
     return total[:n], total[n : n + VN] + total[n + VN :]
+
+
+def agree(weights, pool, beside, *step):
+    terms = as_sent(weights, pool)
+    return as_held(plus(terms, tie(swap(terms, *step), beside)))
 
 
 def dot(a, b, ca=1, cb=0):
@@ -332,8 +339,9 @@
     stored = slow(adj)
     ids = merge(merge(vid[0][None], "core", core), "x", x, 1)
     ids = merge(merge(ids, "x", x, 2), "zl", zl).reshape(dst_blocks, 1, BS)
-    a2, ids = tie((a2, ids), to_dst, to_src)
+    a2, ids = tie((a2, ids))
     b1, b2, b3 = ring(b0, -1), pair(a2), ring(b0, 1)
+    ids = tie(ids, to_dst, to_src)
     q, adj = call(
         q_kernel, (src, tgt_read, count), [stored, ids], [((2 * VN, src_blocks * BS), BF16), (adj.shape, BF16)],
         [pltpu.VMEM((VN, (src_blocks + 1) * BS), F32), pltpu.SemaphoreType.DMA((5,))],
@@ -374,25 +382,26 @@
     weights = jnp.concatenate([dot(grad_pre, mixed, 0, 0), dot(hidden, cotangent[0], 0, 0)])
     layer_out = (dot(hidden, w_out) + mixed.astype(F32)).astype(BF16)
     fan = w_in.shape[1]
+    weights, pool = agree(weights, as_held(pool.astype(F32))[1], layer_out, "zl")
     quads = weights.reshape(4, fan // 2, width)
+    pool = jnp.concatenate(split(pool))
     w0, w1, w2, w3 = [lax.dynamic_index_in_dim(quads, (x + k) % 4, 0, keepdims=False).astype(BF16) for k in range(4)]
-    a2, b0 = tie((a2, b0), layer_out, w1, w2, w3)
+    b0 = tie(b0, layer_out)
+    a2 = tie(a2, w2)
     b1 = ring(jnp.concatenate([b0, w3, pool]), -1)
     b3 = ring(jnp.concatenate([b0, w1, pool]), 1)
     b2 = pair(a2)
     near = send(jnp.concatenate([own, a1, a2, a3, b0]), core=1)
     terms = jnp.concatenate([w0, pool]), ring(jnp.concatenate([w2, pool]), 2), b1[nodes:], b3[nodes:]
-    terms = plus(*terms)
-    deep = fan // 2
-    weights, pool = terms[:deep], terms[deep : deep + VN] + terms[deep + VN :]
-    far = [send(b, core=1) for b in (b1, b2, b3)]
-    weights, pool = agree(weights, pool, "y")
+    terms = as_sent(*as_held(plus(*terms)))
+    far = [send(b, core=1) for b in (b1, jnp.concatenate([b2, terms]), b3)]
+    weights, pool = as_held(plus(terms, far[1][nodes:]))
     panel, adj = call(
         target_kernel, (), [stored, own, a1, a2, a3, b0, b1, b2, b3, near, *far],
         [(((dst_blocks + 1) * BS, part), BF16), (stored.shape, BF16)],
         [pltpu.SemaphoreType.DMA, pltpu.SemaphoreType.DMA((12,))], 0, stored.size * 2, 13,
     )
-    weights, pool, panel = tie((weights, pool, panel))
+    weights, pool, panel = tie((*agree(weights, pool, panel, "y", 2), panel))
 
     ride = nodes // width * VN
     outs = [((nodes + ride, part), BF16)] * 4
@@ -404,22 +413,19 @@
         )
 
     other = backward(1, panel)
-    weights, pool, other = tie((*agree(weights, pool, "zh"), other))
+    weights, pool, other = tie((*agree(weights, pool, other, "y"), other))
     o = scatter_first("row", other)
     own = backward(0, panel)
-    weights, pool, own, o = tie((*agree(weights, pool, "y", 2), own, o))
-    sums = scatter_add(own, other, o)
-    weights, pool = tie((weights, pool), sums)
-    terms = scatter_last("row", own, sums)
-    weights, pool = agree(*agree(weights, pool, "core"), "zl")
+    weights, pool, own, o = tie((*agree(weights, pool, (own, o), "zh"), own, o))
+    terms = scatter_last("row", own, scatter_add(own, other, o))
     weights = tie(weights.astype(BF16), terms[-1])
     for bit in (1, 2):
         weights = merge(weights, "x", x, bit)
+    grad_in = weights[:fan].astype(F32).T
+    grad_out = weights[fan:].astype(F32)
     grad_features = pl.pallas_call(
         final_kernel, out_shape=jax.ShapeDtypeStruct((nodes, part), F32)
-    )(scale * pool, *terms)
-    grad_in = weights[:fan].astype(F32).T
-    grad_out = weights[fan:].astype(F32)
+    )(scale * pool, *[fast(t) for t in terms])
     return (layer_out[None], grad_features[None], grad_in, grad_out)
 
 

time: 253 us -> 234 us (0.925)
  Pallas kernels: 42.6 us -> 34.5 us
  starting transfers between devices: 76.5 us -> 69.8 us
  waiting for transfers between devices: 106 us -> 103 us
    ppermute x16 -> x15, starting transfers between devices: 26.7 us -> 17.2 us  [swap(): lax.ppermute(value, BOTH, [(i, i ^ stride * bit) for i in range(128)])]
    pallas_call x9, Pallas kernels: 39.4 us -> 32.3 us  [call(): pl.pallas_call(kernel, out_shape=[pltpu.VMEM(shape, dtype) for shape, dty...]
    ppermute x34, waiting for transfers between devices: 80.9 us -> 76.2 us  [send(): return lax.ppermute(value, BOTH, route(**step))]
    ppermute x34, starting transfers between devices: 49.8 us -> 52.6 us  [send(): return lax.ppermute(value, BOTH, route(**step))]
    ppermute x16 -> x15, waiting for transfers between devices: 25.5 us -> 26.6 us  [swap(): lax.ppermute(value, BOTH, [(i, i ^ stride * bit) for i in range(128)])]
  transfers between devices with their start and end apart: 50 -> 49, of which waited for: 20 -> 24; matrix products, arithmetic and copies ran while one was open for 7% -> 8% of each run, Pallas kernels for 11% -> 11%
where the time goes in v2:
time: 234 us
  waiting for transfers between devices  103 us (44%)
  starting transfers between devices  69.8 us (30%)
  Pallas kernels  34.5 us (15%)
  other arithmetic  13.8 us (6%)
  local copies, waits for them, and re-layouts  7.44 us (3%)
  matrix products  3.29 us (1%)
    ppermute x34, waiting for transfers between devices, send(): return lax.ppermute(value, BOTH, route(**step))  76.2 us
    ppermute x34, starting transfers between devices, send(): return lax.ppermute(value, BOTH, route(**step))  52.6 us
    pallas_call x9, Pallas kernels, call(): pl.pallas_call(kernel, out_shape=[pltpu.VMEM(shape, dtype) for shape, dty...  32.3 us
    ppermute x15, waiting for transfers between devices, swap(): lax.ppermute(value, BOTH, [(i, i ^ stride * bit) for i in range(128)])  26.6 us
    ppermute x15, starting transfers between devices, swap(): lax.ppermute(value, BOTH, [(i, i ^ stride * bit) for i in range(128)])  17.2 us
  transfers between devices with their start and end apart: 49, of which 24 were waited for; matrix products, arithmetic and copies ran while one was open for 8% of the time, Pallas kernels for 11%

profile of v2, /device:TPU:1, one launch (start us, length us, event | category | flops | bytes accessed | tf_op | source)
XLA Modules:
  0.0 233.6 jit_solution(6050173832118805619)
XLA Ops:
  0.6 3.8 %collective-permute-start = (bf16[1024,256]{1,0:T(8,128)(2,1)}, bf16[1024,256]{1,0:T(8,128)(2,1)S(1)}, u32[]{:S(2)}, u32[]{:S(2)}) collective-permute-start(bf16[1024,256]{1,0:T(8,128)(2,1)} %bitcast.32), channel_id=1, source_target_pairs={{0,32},{1,33},{2,34},{3,35},{4,36},{5,37},{6,38},{7,39},{8,40},{9,... | collective-permute-start | bytes 1572872 | tf_op jit(solution)/shard_map/ppermute | solution.py:31
  4.5 3.6 %collective-permute-start.7 = (bf16[1024,256]{1,0:T(8,128)(2,1)}, bf16[1024,256]{1,0:T(8,128)(2,1)S(1)}, u32[]{:S(2)}, u32[]{:S(2)}) collective-permute-start(bf16[1024,256]{1,0:T(8,128)(2,1)} %bitcast.33), channel_id=1, source_target_pairs={{0,64},{1,65},{2,66},{3,67},{4,68},{5,69},{6,70},{7,71},{8,72},{9,... | collective-permute-start | bytes 1572872 | tf_op jit(solution)/shard_map/ppermute | solution.py:31
  21.1 2.8 %collective-permute-start.3 = (s32[4,1024]{1,0:T(4,128)S(1)}, s32[4,1024]{1,0:T(4,128)S(1)}, u32[]{:S(2)}, u32[]{:S(2)}) collective-permute-start(s32[4,1024]{1,0:T(4,128)S(1)} %add_select_fusion.2), channel_id=1, source_target_pairs={{0,4},{1,5},{2,6},{3,7},{4,0},{5,1},{6,2},{7,3},{8,12},{9,13},{10,... | collective-permute-start | bytes 49160 | tf_op jit(solution)/shard_map/ppermute | solution.py:36
  26.7 3.2 %stack.13.ends = s32[5]{0:T(128)S(1)} concatenate(s32[1]{0:T(128)} %get-tuple-element.198, s32[1]{0:T(128)} %get-tuple-element.197, s32[1]{0:T(128)} %get-tuple-element.196, s32[1]{0:T(128)} %get-tuple-element.195, s32[1]{0:T(128)} %bitcast.4), dimensions={0} | concatenate | bytes 40 | tf_op jit(solution)/shard_map/stack | solution.py:276
  35.7 5.7 %shard_map.120 = (bf16[32,8192]{1,0:T(8,128)(2,1)S(1)}, bf16[320,128,128]{2,1,0:T(8,128)(2,1)S(1)}) custom-call(s32[320]{0:T(512)S(1)} %get-tuple-element.161.src, s32[320]{0:T(512)S(1)} %get-tuple-element.192.dst, s32[1]{0:T(128)} %bitcast.31.live, bf16[320,128,128]{2,1,0:T(8,128)(2,1)} %bitcast.38, s32[128,1,128]{2,1,0:T(1,128)S(1)} %select_n.380.ids), custom_call_target="tpu_custom_call" | custom-call | flops 167772160 | bytes 10485760 | tf_op jit(solution)/shard_map/pallas_call | solution.py:134
  43.9 5.1 %shard_map.122 = bf16[8192,256]{1,0:T(8,128)(2,1)S(1)} custom-call(s32[288]{0:T(512)S(1)} %get-tuple-element.143.c0, s32[288]{0:T(512)S(1)} %get-tuple-element.142.c1, s32[288]{0:T(512)S(1)} %multiply_add_fusion.to, s32[5]{0:T(128)S(1)} %stack.13.ends, bf16[320,128,128]{2,1,0:T(8,128)(2,1)S(1)} %get-tuple-element.76.adj, ...), custom_call_target="tpu_custom_call" | custom-call | flops 1342177280 | bytes 5242880 | tf_op jit(solution)/shard_map/pallas_call | solution.py:134
  49.0 7.0 %collective-permute-start.13 = (bf16[8192,256]{1,0:T(8,128)(2,1)S(1)}, bf16[8192,256]{1,0:T(8,128)(2,1)S(1)}, u32[]{:S(2)}, u32[]{:S(2)}) collective-permute-start(bf16[8192,256]{1,0:T(8,128)(2,1)S(1)} %shard_map.122), channel_id=1, source_target_pairs={{0,1},{1,0},{2,3},{3,2},{4,5},{5,4},{6,7},{7,6},{8,9},{9,8},{10,11... | collective-permute-start | bytes 12582920 | tf_op jit(solution)/shard_map/ppermute | solution.py:31
  56.1 2.6 %collective-permute-done.11 = f32[16,256]{1,0:T(8,128)S(1)} collective-permute-done((f32[16,256]{1,0:T(8,128)S(1)}, f32[16,256]{1,0:T(8,128)S(1)}, u32[]{:S(2)}, u32[]{:S(2)}) %collective-permute-start.11) | collective-permute-done | bytes 16416 | tf_op jit(solution)/shard_map/ppermute | solution.py:36
  58.7 2.8 %shard_map.123 = bf16[4096,256]{1,0:T(8,128)(2,1)S(1)} custom-call(s32[288]{0:T(512)S(1)} %get-tuple-element.143.c0, s32[288]{0:T(512)S(1)} %get-tuple-element.142.c1, s32[288]{0:T(512)S(1)} %multiply_add_fusion.to, s32[5]{0:T(128)S(1)} %stack.13.ends, bf16[320,128,128]{2,1,0:T(8,128)(2,1)S(1)} %get-tuple-element.76.adj, ...), custom_call_target="tpu_custom_call" | custom-call | flops 1342177280 | bytes 5242880 | tf_op jit(solution)/shard_map/pallas_call | solution.py:134
  64.4 2.7 %collective-permute-start.18 = (bf16[1024,256]{1,0:T(8,128)(2,1)S(1)}, bf16[1024,256]{1,0:T(8,128)(2,1)S(1)}, u32[]{:S(2)}, u32[]{:S(2)}) collective-permute-start(bf16[1024,256]{1,0:T(8,128)(2,1)S(1)} %get-tuple-element.170), channel_id=1, source_target_pairs={{0,6},{1,7},{2,0},{3,1},{4,2},{5,3},{6,4},{7,5},{8,14},{9,15},{10,... | collective-permute-start | bytes 1572872 | tf_op jit(solution)/shard_map/ppermute | solution.py:31
  67.3 2.8 %shard_map.124 = bf16[4096,256]{1,0:T(8,128)(2,1)S(1)} custom-call(s32[288]{0:T(512)S(1)} %get-tuple-element.143.c0, s32[288]{0:T(512)S(1)} %get-tuple-element.142.c1, s32[288]{0:T(512)S(1)} %multiply_add_fusion.to, s32[5]{0:T(128)S(1)} %stack.13.ends, bf16[320,128,128]{2,1,0:T(8,128)(2,1)S(1)} %get-tuple-element.76.adj, ...), custom_call_target="tpu_custom_call" | custom-call | flops 1342177280 | bytes 5242880 | tf_op jit(solution)/shard_map/pallas_call | solution.py:134
  71.7 2.6 %collective-permute-done.15 = f32[16,256]{1,0:T(8,128)S(1)} collective-permute-done((f32[16,256]{1,0:T(8,128)S(1)}, f32[16,256]{1,0:T(8,128)S(1)}, u32[]{:S(2)}, u32[]{:S(2)}) %collective-permute-start.15) | collective-permute-done | bytes 16416 | tf_op jit(solution)/shard_map/ppermute | solution.py:36
  74.3 4.7 %collective-permute-start.16 = (f32[16,256]{1,0:T(8,128)S(1)}, f32[16,256]{1,0:T(8,128)S(1)}, u32[]{:S(2)}, u32[]{:S(2)}) collective-permute-start(f32[16,256]{1,0:T(8,128)S(1)} %add.504), channel_id=1, source_target_pairs={{0,1},{1,0},{2,3},{3,2},{4,5},{5,4},{6,7},{7,6},{8,9},{9,8},{10,11... | collective-permute-start | bytes 49160 | tf_op jit(solution)/shard_map/ppermute | solution.py:36
  85.4 10.1 %collective-permute-done.20.refs_1_ = bf16[1056,256]{1,0:T(8,128)(2,1)S(1)} collective-permute-done((bf16[1056,256]{1,0:T(8,128)(2,1)S(1)}, bf16[1056,256]{1,0:T(8,128)(2,1)S(1)}, u32[]{:S(2)}, u32[]{:S(2)}) %collective-permute-start.20) | collective-permute-done | bytes 540704 | tf_op jit(solution)/shard_map/ppermute | solution.py:31
  95.5 9.7 %collective-permute-done.21.refs_2_ = bf16[1056,256]{1,0:T(8,128)(2,1)S(1)} collective-permute-done((bf16[1056,256]{1,0:T(8,128)(2,1)S(1)}, bf16[1056,256]{1,0:T(8,128)(2,1)S(1)}, u32[]{:S(2)}, u32[]{:S(2)}) %collective-permute-start.21) | collective-permute-done | bytes 540704 | tf_op jit(solution)/shard_map/ppermute | solution.py:31
  105.2 2.5 %collective-permute-done.22.refs_3_ = bf16[1056,256]{1,0:T(8,128)(2,1)S(1)} collective-permute-done((bf16[1056,256]{1,0:T(8,128)(2,1)S(1)}, bf16[1056,256]{1,0:T(8,128)(2,1)S(1)}, u32[]{:S(2)}, u32[]{:S(2)}) %collective-permute-start.22) | collective-permute-done | bytes 540704 | tf_op jit(solution)/shard_map/ppermute | solution.py:31
  107.7 2.8 %shard_map.125 = (bf16[1024,256]{1,0:T(8,128)(2,1)S(1)}, bf16[1024,512]{1,0:T(8,128)(2,1)S(1)}, bf16[1024,512]{1,0:T(8,128)(2,1)S(1)}, bf16[1024,256]{1,0:T(8,128)(2,1)S(1)}, bf16[32,256]{1,0:T(8,128)(2,1)S(1)}) custom-call(s32[1,1024]{1,0:T(1,128)S(1)} %copy-done.5, f32[16,256]{1,0:T(8,128)S(1)} %fusion.14.pooled, bf16[256,512]{1,0:T(8,128)(2,1)S(1)} %copy-done.4, ...), custom_call_target="tpu_custom_call" | custom-call | flops 805306368 | bytes 2097152 | tf_op jit(solution)/shard_map/pallas_call | solution.py:134
  110.5 3.4 %collective-permute-start.33 = (bf16[1024,256]{1,0:T(8,128)(2,1)S(1)}, bf16[1024,256]{1,0:T(8,128)(2,1)S(1)}, u32[]{:S(2)}, u32[]{:S(2)}) collective-permute-start(bf16[1024,256]{1,0:T(8,128)(2,1)S(1)} %get-tuple-element.95.refs_0_), channel_id=1, source_target_pairs={{0,6},{1,7},{2,0},{3,1},{4,2},{5,3},{6,4},{7,5},{8,14},{9,15},{10,... | collective-permute-start | bytes 1572872 | tf_op jit(solution)/shard_map/ppermute | solution.py:31
  121.0 5.6 %collective-permute-done.26.refs_4_ = bf16[1024,256]{1,0:T(8,128)(2,1)S(1)} collective-permute-done((bf16[1024,256]{1,0:T(8,128)(2,1)S(1)}, bf16[1024,256]{1,0:T(8,128)(2,1)S(1)}, u32[]{:S(2)}, u32[]{:S(2)}) %collective-permute-start.26) | collective-permute-done | bytes 524320 | tf_op jit(solution)/shard_map/ppermute | solution.py:31
  126.6 9.2 %collective-permute-done.33.refs_1_ = bf16[1024,256]{1,0:T(8,128)(2,1)S(1)} collective-permute-done((bf16[1024,256]{1,0:T(8,128)(2,1)S(1)}, bf16[1024,256]{1,0:T(8,128)(2,1)S(1)}, u32[]{:S(2)}, u32[]{:S(2)}) %collective-permute-start.33) | collective-permute-done | bytes 524320 | tf_op jit(solution)/shard_map/ppermute | solution.py:31
  135.9 2.4 %collective-permute-done.24 = bf16[1056,256]{1,0:T(8,128)(2,1)} collective-permute-done((bf16[1056,256]{1,0:T(8,128)(2,1)}, bf16[1056,256]{1,0:T(8,128)(2,1)}, u32[]{:S(2)}, u32[]{:S(2)}) %collective-permute-start.24) | collective-permute-done | bytes 540704 | tf_op jit(solution)/shard_map/ppermute | solution.py:36
  141.3 2.6 %collective-permute-done.34.refs_3_ = bf16[1024,256]{1,0:T(8,128)(2,1)S(1)} collective-permute-done((bf16[1024,256]{1,0:T(8,128)(2,1)S(1)}, bf16[1024,256]{1,0:T(8,128)(2,1)S(1)}, u32[]{:S(2)}, u32[]{:S(2)}) %collective-permute-start.34) | collective-permute-done | bytes 524320 | tf_op jit(solution)/shard_map/ppermute | solution.py:31
  146.8 14.3 %collective-permute-done.25 = bf16[288,256]{1,0:T(8,128)(2,1)S(1)} collective-permute-done((bf16[288,256]{1,0:T(8,128)(2,1)S(1)}, bf16[288,256]{1,0:T(8,128)(2,1)S(1)}, u32[]{:S(2)}, u32[]{:S(2)}) %collective-permute-start.25) | collective-permute-done | bytes 147488 | tf_op jit(solution)/shard_map/ppermute | solution.py:31
  166.8 4.1 %shard_map.126 = (bf16[16512,256]{1,0:T(8,128)(2,1)S(1)}, bf16[320,128,128]{2,1,0:T(8,128)(2,1)S(1)}) custom-call(bf16[320,128,128]{2,1,0:T(8,128)(2,1)} %bitcast.39, bf16[1024,256]{1,0:T(8,128)(2,1)S(1)} %get-tuple-element.95.refs_0_, bf16[1024,256]{1,0:T(8,128)(2,1)S(1)} %collective-permute-done.33.refs_1_, ...), custom_call_target="tpu_custom_call" | custom-call | bytes 10485760 | tf_op jit(solution)/shard_map/pallas_call | solution.py:134
  172.3 3.8 %shard_map.127 = (bf16[1088,256]{1,0:T(8,128)(2,1)S(1)}, bf16[1088,256]{1,0:T(8,128)(2,1)S(1)}, bf16[1088,256]{1,0:T(8,128)(2,1)S(1)}, bf16[1088,256]{1,0:T(8,128)(2,1)S(1)}) custom-call(s32[224]{0:T(256)S(1)} %get-tuple-element.145.c0, s32[224]{0:T(256)S(1)} %get-tuple-element.144.c1, s32[224]{0:T(256)S(1)} %multiply_add_fusion.1.to, ...), custom_call_target="tpu_custom_call" | custom-call | flops 1342177280 | bytes 5242880 | tf_op jit(solution)/shard_map/pallas_call | solution.py:134
  178.9 4.1 %collective-permute-start.42 = (bf16[1088,256]{1,0:T(8,128)(2,1)S(1)}, bf16[1088,256]{1,0:T(8,128)(2,1)S(1)}, u32[]{:S(2)}, u32[]{:S(2)}) collective-permute-start(bf16[1088,256]{1,0:T(8,128)(2,1)S(1)} %get-tuple-element.117), channel_id=1, source_target_pairs={{0,64},{1,65},{2,66},{3,67},{4,68},{5,69},{6,70},{7,71},{8,72},{9,... | collective-permute-start | bytes 1671176 | tf_op jit(solution)/shard_map/ppermute | solution.py:31
  183.3 4.3 %shard_map.128 = (bf16[1088,256]{1,0:T(8,128)(2,1)S(1)}, bf16[1088,256]{1,0:T(8,128)(2,1)S(1)}, bf16[1088,256]{1,0:T(8,128)(2,1)S(1)}, bf16[1088,256]{1,0:T(8,128)(2,1)S(1)}) custom-call(s32[224]{0:T(256)S(1)} %get-tuple-element.145.c0, s32[224]{0:T(256)S(1)} %get-tuple-element.144.c1, s32[224]{0:T(256)S(1)} %multiply_add_fusion.1.to, ...), custom_call_target="tpu_custom_call" | custom-call | flops 1342177280 | bytes 5242880 | tf_op jit(solution)/shard_map/pallas_call | solution.py:134
  187.7 9.8 %collective-permute-done.39 = bf16[288,256]{1,0:T(8,128)(2,1)S(1)} collective-permute-done((bf16[288,256]{1,0:T(8,128)(2,1)S(1)}, bf16[288,256]{1,0:T(8,128)(2,1)S(1)}, u32[]{:S(2)}, u32[]{:S(2)}) %collective-permute-start.39) | collective-permute-done | bytes 147488 | tf_op jit(solution)/shard_map/ppermute | solution.py:36
  197.7 3.8 %collective-permute-start.46 = (bf16[1088,256]{1,0:T(8,128)(2,1)S(1)}, bf16[1088,256]{1,0:T(8,128)(2,1)S(1)}, u32[]{:S(2)}, u32[]{:S(2)}) collective-permute-start(bf16[1088,256]{1,0:T(8,128)(2,1)S(1)} %add_convert_fusion), channel_id=1, source_target_pairs={{0,64},{1,65},{2,66},{3,67},{4,68},{5,69},{6,70},{7,71},{8,72},{9,... | collective-permute-start | bytes 1671176 | tf_op jit(solution)/shard_map/ppermute | solution.py:31
  204.5 8.1 %collective-permute-done.46.refs_4_ = bf16[1088,256]{1,0:T(8,128)(2,1)S(1)} collective-permute-done((bf16[1088,256]{1,0:T(8,128)(2,1)S(1)}, bf16[1088,256]{1,0:T(8,128)(2,1)S(1)}, u32[]{:S(2)}, u32[]{:S(2)}) %collective-permute-start.46) | collective-permute-done | bytes 557088 | tf_op jit(solution)/shard_map/ppermute | solution.py:31
  212.6 4.1 %collective-permute-done.47 = bf16[256,256]{1,0:T(8,128)(2,1)S(1)} collective-permute-done((bf16[256,256]{1,0:T(8,128)(2,1)S(1)}, bf16[256,256]{1,0:T(8,128)(2,1)S(1)}, u32[]{:S(2)}, u32[]{:S(2)}) %collective-permute-start.47) | collective-permute-done | bytes 131104 | tf_op jit(solution)/shard_map/ppermute | solution.py:36
  219.0 10.3 %collective-permute-done.43.refs_1_ = bf16[1088,256]{1,0:T(8,128)(2,1)S(1)} collective-permute-done((bf16[1088,256]{1,0:T(8,128)(2,1)S(1)}, bf16[1088,256]{1,0:T(8,128)(2,1)S(1)}, u32[]{:S(2)}, u32[]{:S(2)}) %collective-permute-start.43) | collective-permute-done | bytes 557088 | tf_op jit(solution)/shard_map/ppermute | solution.py:31
  (190 shorter events, 67.0 us)
Async XLA Ops:
  0.6 29.4 %collective-permute-start = (bf16[1024,256]{1,0:T(8,128)(2,1)}, bf16[1024,256]{1,0:T(8,128)(2,1)S(1)}, u32[]{:S(2)}, u32[]{:S(2)}) collective-permute-start(bf16[1024,256]{1,0:T(8,128)(2,1)} %bitcast.32), channel_id=1, source_target_pairs={{0,32},{1,33},{2,34},{3,35},{4,36},{5,37},{6,38},{7,39},{8,40},{9,... | collective-permute-start | bytes 1572872 | tf_op jit(solution)/shard_map/ppermute | solution.py:31
  4.5 26.6 %collective-permute-start.7 = (bf16[1024,256]{1,0:T(8,128)(2,1)}, bf16[1024,256]{1,0:T(8,128)(2,1)S(1)}, u32[]{:S(2)}, u32[]{:S(2)}) collective-permute-start(bf16[1024,256]{1,0:T(8,128)(2,1)} %bitcast.33), channel_id=1, source_target_pairs={{0,64},{1,65},{2,66},{3,67},{4,68},{5,69},{6,70},{7,71},{8,72},{9,... | collective-permute-start | bytes 1572872 | tf_op jit(solution)/shard_map/ppermute | solution.py:31
  8.1 35.0 %collective-permute-start.5 = (bf16[1024,256]{1,0:T(8,128)(2,1)}, bf16[1024,256]{1,0:T(8,128)(2,1)S(1)}, u32[]{:S(2)}, u32[]{:S(2)}) collective-permute-start(bf16[1024,256]{1,0:T(8,128)(2,1)} %bitcast.34), channel_id=1, source_target_pairs={{0,48},{1,49},{2,50},{3,51},{4,52},{5,53},{6,54},{7,55},{8,56},{9,... | collective-permute-start | bytes 1572872 | tf_op jit(solution)/shard_map/ppermute | solution.py:31
  8.8 34.2 %collective-permute-start.6 = (bf16[1024,256]{1,0:T(8,128)(2,1)}, bf16[1024,256]{1,0:T(8,128)(2,1)S(1)}, u32[]{:S(2)}, u32[]{:S(2)}) collective-permute-start(bf16[1024,256]{1,0:T(8,128)(2,1)} %bitcast.35), channel_id=1, source_target_pairs={{0,16},{1,17},{2,18},{3,19},{4,20},{5,21},{6,22},{7,23},{8,24},{9,... | collective-permute-start | bytes 1572872 | tf_op jit(solution)/shard_map/ppermute | solution.py:31
  30.0 12.7 %collective-permute-start.9 = (bf16[1024,256]{1,0:T(8,128)(2,1)S(1)}, bf16[1024,256]{1,0:T(8,128)(2,1)S(1)}, u32[]{:S(2)}, u32[]{:S(2)}) collective-permute-start(bf16[1024,256]{1,0:T(8,128)(2,1)S(1)} %collective-permute-done.refs_2_), channel_id=1, source_target_pairs={{0,64},{1,65},{2,66},{3,67},{4,68},{5,69},{6,70},{7,71},{8,72},{9,... | collective-permute-start | bytes 1572872 | tf_op jit(solution)/shard_map/ppermute | solution.py:31
  49.0 13.8 %collective-permute-start.13 = (bf16[8192,256]{1,0:T(8,128)(2,1)S(1)}, bf16[8192,256]{1,0:T(8,128)(2,1)S(1)}, u32[]{:S(2)}, u32[]{:S(2)}) collective-permute-start(bf16[8192,256]{1,0:T(8,128)(2,1)S(1)} %shard_map.122), channel_id=1, source_target_pairs={{0,1},{1,0},{2,3},{3,2},{4,5},{5,4},{6,7},{7,6},{8,9},{9,8},{10,11... | collective-permute-start | bytes 12582920 | tf_op jit(solution)/shard_map/ppermute | solution.py:31
  63.5 16.4 %collective-permute-start.17 = (bf16[1024,256]{1,0:T(8,128)(2,1)S(1)}, bf16[1024,256]{1,0:T(8,128)(2,1)S(1)}, u32[]{:S(2)}, u32[]{:S(2)}) collective-permute-start(bf16[1024,256]{1,0:T(8,128)(2,1)S(1)} %get-tuple-element.172), channel_id=1, source_target_pairs={{0,2},{1,3},{2,4},{3,5},{4,6},{5,7},{6,0},{7,1},{8,10},{9,11},{10,... | collective-permute-start | bytes 1572872 | tf_op jit(solution)/shard_map/ppermute | solution.py:31
  64.4 15.4 %collective-permute-start.18 = (bf16[1024,256]{1,0:T(8,128)(2,1)S(1)}, bf16[1024,256]{1,0:T(8,128)(2,1)S(1)}, u32[]{:S(2)}, u32[]{:S(2)}) collective-permute-start(bf16[1024,256]{1,0:T(8,128)(2,1)S(1)} %get-tuple-element.170), channel_id=1, source_target_pairs={{0,6},{1,7},{2,0},{3,1},{4,2},{5,3},{6,4},{7,5},{8,14},{9,15},{10,... | collective-permute-start | bytes 1572872 | tf_op jit(solution)/shard_map/ppermute | solution.py:31
  67.1 12.8 %collective-permute-start.19 = (bf16[1024,256]{1,0:T(8,128)(2,1)S(1)}, bf16[1024,256]{1,0:T(8,128)(2,1)S(1)}, u32[]{:S(2)}, u32[]{:S(2)}) collective-permute-start(bf16[1024,256]{1,0:T(8,128)(2,1)S(1)} %get-tuple-element.171), channel_id=1, source_target_pairs={{0,8},{1,9},{2,10},{3,11},{4,12},{5,13},{6,14},{7,15},{8,0},{9,1},... | collective-permute-start | bytes 1572872 | tf_op jit(solution)/shard_map/ppermute | solution.py:31
  80.9 14.7 %collective-permute-start.20 = (bf16[1056,256]{1,0:T(8,128)(2,1)S(1)}, bf16[1056,256]{1,0:T(8,128)(2,1)S(1)}, u32[]{:S(2)}, u32[]{:S(2)}) collective-permute-start(bf16[1056,256]{1,0:T(8,128)(2,1)S(1)} %get-tuple-element.189), channel_id=1, source_target_pairs={{0,2},{1,3},{2,4},{3,5},{4,6},{5,7},{6,0},{7,1},{8,10},{9,11},{10,... | collective-permute-start | bytes 1622024 | tf_op jit(solution)/shard_map/ppermute | solution.py:31
  81.1 24.1 %collective-permute-start.21 = (bf16[1056,256]{1,0:T(8,128)(2,1)S(1)}, bf16[1056,256]{1,0:T(8,128)(2,1)S(1)}, u32[]{:S(2)}, u32[]{:S(2)}) collective-permute-start(bf16[1056,256]{1,0:T(8,128)(2,1)S(1)} %get-tuple-element.188), channel_id=1, source_target_pairs={{0,4},{1,5},{2,6},{3,7},{4,0},{5,1},{6,2},{7,3},{8,12},{9,13},{10,... | collective-permute-start | bytes 1622024 | tf_op jit(solution)/shard_map/ppermute | solution.py:31
  83.2 24.4 %collective-permute-start.22 = (bf16[1056,256]{1,0:T(8,128)(2,1)S(1)}, bf16[1056,256]{1,0:T(8,128)(2,1)S(1)}, u32[]{:S(2)}, u32[]{:S(2)}) collective-permute-start(bf16[1056,256]{1,0:T(8,128)(2,1)S(1)} %get-tuple-element.187), channel_id=1, source_target_pairs={{0,6},{1,7},{2,0},{3,1},{4,2},{5,3},{6,4},{7,5},{8,14},{9,15},{10,... | collective-permute-start | bytes 1622024 | tf_op jit(solution)/shard_map/ppermute | solution.py:31
  84.5 23.2 %collective-permute-start.23 = (bf16[1024,256]{1,0:T(8,128)(2,1)S(1)}, bf16[1024,256]{1,0:T(8,128)(2,1)S(1)}, u32[]{:S(2)}, u32[]{:S(2)}) collective-permute-start(bf16[1024,256]{1,0:T(8,128)(2,1)S(1)} %add_convert_fusion.2), channel_id=1, source_target_pairs={{0,8},{1,9},{2,10},{3,11},{4,12},{5,13},{6,14},{7,15},{8,0},{9,1},... | collective-permute-start | bytes 1572872 | tf_op jit(solution)/shard_map/ppermute | solution.py:31
  110.5 25.3 %collective-permute-start.33 = (bf16[1024,256]{1,0:T(8,128)(2,1)S(1)}, bf16[1024,256]{1,0:T(8,128)(2,1)S(1)}, u32[]{:S(2)}, u32[]{:S(2)}) collective-permute-start(bf16[1024,256]{1,0:T(8,128)(2,1)S(1)} %get-tuple-element.95.refs_0_), channel_id=1, source_target_pairs={{0,6},{1,7},{2,0},{3,1},{4,2},{5,3},{6,4},{7,5},{8,14},{9,15},{10,... | collective-permute-start | bytes 1572872 | tf_op jit(solution)/shard_map/ppermute | solution.py:31
  113.9 12.7 %collective-permute-start.26 = (bf16[1024,256]{1,0:T(8,128)(2,1)S(1)}, bf16[1024,256]{1,0:T(8,128)(2,1)S(1)}, u32[]{:S(2)}, u32[]{:S(2)}) collective-permute-start(bf16[1024,256]{1,0:T(8,128)(2,1)S(1)} %get-tuple-element.95.refs_0_), channel_id=1, source_target_pairs={{0,8},{1,9},{2,10},{3,11},{4,12},{5,13},{6,14},{7,15},{8,0},{9,1},... | collective-permute-start | bytes 1572872 | tf_op jit(solution)/shard_map/ppermute | solution.py:31
  117.3 21.0 %collective-permute-start.24 = (bf16[1056,256]{1,0:T(8,128)(2,1)}, bf16[1056,256]{1,0:T(8,128)(2,1)}, u32[]{:S(2)}, u32[]{:S(2)}) collective-permute-start(bf16[1056,256]{1,0:T(8,128)(2,1)} %pad_maximum_fusion.13), channel_id=1, source_target_pairs={{0,8},{1,9},{2,10},{3,11},{4,12},{5,13},{6,14},{7,15},{8,0},{9,1},... | collective-permute-start | bytes 1622024 | tf_op jit(solution)/shard_map/ppermute | solution.py:36
  118.0 21.7 %collective-permute-start.29 = (bf16[1024,256]{1,0:T(8,128)(2,1)S(1)}, bf16[1024,256]{1,0:T(8,128)(2,1)S(1)}, u32[]{:S(2)}, u32[]{:S(2)}) collective-permute-start(bf16[1024,256]{1,0:T(8,128)(2,1)S(1)} %get-tuple-element.95.refs_0_), channel_id=1, source_target_pairs={{0,4},{1,5},{2,6},{3,7},{4,0},{5,1},{6,2},{7,3},{8,12},{9,13},{10,... | collective-permute-start | bytes 1572872 | tf_op jit(solution)/shard_map/ppermute | solution.py:31
  118.0 25.9 %collective-permute-start.34 = (bf16[1024,256]{1,0:T(8,128)(2,1)S(1)}, bf16[1024,256]{1,0:T(8,128)(2,1)S(1)}, u32[]{:S(2)}, u32[]{:S(2)}) collective-permute-start(bf16[1024,256]{1,0:T(8,128)(2,1)S(1)} %get-tuple-element.95.refs_0_), channel_id=1, source_target_pairs={{0,2},{1,3},{2,4},{3,5},{4,6},{5,7},{6,0},{7,1},{8,10},{9,11},{10,... | collective-permute-start | bytes 1572872 | tf_op jit(solution)/shard_map/ppermute | solution.py:31
  139.7 21.3 %collective-permute-start.27 = (bf16[1312,256]{1,0:T(8,128)(2,1)S(1)}, bf16[1312,256]{1,0:T(8,128)(2,1)S(1)}, u32[]{:S(2)}, u32[]{:S(2)}) collective-permute-start(bf16[1312,256]{1,0:T(8,128)(2,1)S(1)} %get-tuple-element.174), channel_id=1, source_target_pairs={{0,6},{1,7},{2,0},{3,1},{4,2},{5,3},{6,4},{7,5},{8,14},{9,15},{10,... | collective-permute-start | bytes 2015240 | tf_op jit(solution)/shard_map/ppermute | solution.py:31
  141.0 20.1 %collective-permute-start.28 = (bf16[1312,256]{1,0:T(8,128)(2,1)S(1)}, bf16[1312,256]{1,0:T(8,128)(2,1)S(1)}, u32[]{:S(2)}, u32[]{:S(2)}) collective-permute-start(bf16[1312,256]{1,0:T(8,128)(2,1)S(1)} %get-tuple-element.175), channel_id=1, source_target_pairs={{0,2},{1,3},{2,4},{3,5},{4,6},{5,7},{6,0},{7,1},{8,10},{9,11},{10,... | collective-permute-start | bytes 2015240 | tf_op jit(solution)/shard_map/ppermute | solution.py:31
  144.0 22.8 %collective-permute-start.35 = (bf16[5120,256]{1,0:T(8,128)(2,1)S(1)}, bf16[5120,256]{1,0:T(8,128)(2,1)S(1)}, u32[]{:S(2)}, u32[]{:S(2)}) collective-permute-start(bf16[5120,256]{1,0:T(8,128)(2,1)S(1)} %constant_dynamic-update-slice_fusion), channel_id=1, source_target_pairs={{0,1},{1,0},{2,3},{3,2},{4,5},{5,4},{6,7},{7,6},{8,9},{9,8},{10,11... | collective-permute-start | bytes 7864328 | tf_op jit(solution)/shard_map/ppermute | solution.py:31
  144.9 16.1 %collective-permute-start.25 = (bf16[288,256]{1,0:T(8,128)(2,1)S(1)}, bf16[288,256]{1,0:T(8,128)(2,1)S(1)}, u32[]{:S(2)}, u32[]{:S(2)}) collective-permute-start(bf16[288,256]{1,0:T(8,128)(2,1)S(1)} %pad_maximum_fusion.14), channel_id=1, source_target_pairs={{0,4},{1,5},{2,6},{3,7},{4,0},{5,1},{6,2},{7,3},{8,12},{9,13},{10,... | collective-permute-start | bytes 442376 | tf_op jit(solution)/shard_map/ppermute | solution.py:31
  145.8 15.4 %collective-permute-start.30 = (bf16[1024,256]{1,0:T(8,128)(2,1)S(1)}, bf16[1024,256]{1,0:T(8,128)(2,1)S(1)}, u32[]{:S(2)}, u32[]{:S(2)}) collective-permute-start(bf16[1024,256]{1,0:T(8,128)(2,1)S(1)} %collective-permute-done.29.refs_2_), channel_id=1, source_target_pairs={{0,8},{1,9},{2,10},{3,11},{4,12},{5,13},{6,14},{7,15},{8,0},{9,1},... | collective-permute-start | bytes 1572872 | tf_op jit(solution)/shard_map/ppermute | solution.py:31
  176.1 21.3 %collective-permute-start.40 = (bf16[1088,256]{1,0:T(8,128)(2,1)S(1)}, bf16[1088,256]{1,0:T(8,128)(2,1)S(1)}, u32[]{:S(2)}, u32[]{:S(2)}) collective-permute-start(bf16[1088,256]{1,0:T(8,128)(2,1)S(1)} %get-tuple-element.115), channel_id=1, source_target_pairs={{0,16},{1,17},{2,18},{3,19},{4,20},{5,21},{6,22},{7,23},{8,24},{9,... | collective-permute-start | bytes 1671176 | tf_op jit(solution)/shard_map/ppermute | solution.py:31
  178.3 19.2 %collective-permute-start.41 = (bf16[1088,256]{1,0:T(8,128)(2,1)S(1)}, bf16[1088,256]{1,0:T(8,128)(2,1)S(1)}, u32[]{:S(2)}, u32[]{:S(2)}) collective-permute-start(bf16[1088,256]{1,0:T(8,128)(2,1)S(1)} %get-tuple-element.116), channel_id=1, source_target_pairs={{0,48},{1,49},{2,50},{3,51},{4,52},{5,53},{6,54},{7,55},{8,56},{9,... | collective-permute-start | bytes 1671176 | tf_op jit(solution)/shard_map/ppermute | solution.py:31
  178.9 18.6 %collective-permute-start.42 = (bf16[1088,256]{1,0:T(8,128)(2,1)S(1)}, bf16[1088,256]{1,0:T(8,128)(2,1)S(1)}, u32[]{:S(2)}, u32[]{:S(2)}) collective-permute-start(bf16[1088,256]{1,0:T(8,128)(2,1)S(1)} %get-tuple-element.117), channel_id=1, source_target_pairs={{0,64},{1,65},{2,66},{3,67},{4,68},{5,69},{6,70},{7,71},{8,72},{9,... | collective-permute-start | bytes 1671176 | tf_op jit(solution)/shard_map/ppermute | solution.py:31
  183.0 14.4 %collective-permute-start.39 = (bf16[288,256]{1,0:T(8,128)(2,1)S(1)}, bf16[288,256]{1,0:T(8,128)(2,1)S(1)}, u32[]{:S(2)}, u32[]{:S(2)}) collective-permute-start(bf16[288,256]{1,0:T(8,128)(2,1)S(1)} %pad_maximum_fusion.20), channel_id=1, source_target_pairs={{0,64},{1,65},{2,66},{3,67},{4,68},{5,69},{6,70},{7,71},{8,72},{9,... | collective-permute-start | bytes 442376 | tf_op jit(solution)/shard_map/ppermute | solution.py:36
  197.7 14.9 %collective-permute-start.46 = (bf16[1088,256]{1,0:T(8,128)(2,1)S(1)}, bf16[1088,256]{1,0:T(8,128)(2,1)S(1)}, u32[]{:S(2)}, u32[]{:S(2)}) collective-permute-start(bf16[1088,256]{1,0:T(8,128)(2,1)S(1)} %add_convert_fusion), channel_id=1, source_target_pairs={{0,64},{1,65},{2,66},{3,67},{4,68},{5,69},{6,70},{7,71},{8,72},{9,... | collective-permute-start | bytes 1671176 | tf_op jit(solution)/shard_map/ppermute | solution.py:31
  201.7 17.3 %collective-permute-start.44 = (bf16[1088,256]{1,0:T(8,128)(2,1)S(1)}, bf16[1088,256]{1,0:T(8,128)(2,1)S(1)}, u32[]{:S(2)}, u32[]{:S(2)}) collective-permute-start(bf16[1088,256]{1,0:T(8,128)(2,1)S(1)} %add_convert_fusion.1), channel_id=1, source_target_pairs={{0,32},{1,33},{2,34},{3,35},{4,36},{5,37},{6,38},{7,39},{8,40},{9,... | collective-permute-start | bytes 1671176 | tf_op jit(solution)/shard_map/ppermute | solution.py:31
  201.8 27.6 %collective-permute-start.43 = (bf16[1088,256]{1,0:T(8,128)(2,1)S(1)}, bf16[1088,256]{1,0:T(8,128)(2,1)S(1)}, u32[]{:S(2)}, u32[]{:S(2)}) collective-permute-start(bf16[1088,256]{1,0:T(8,128)(2,1)S(1)} %get-tuple-element.121), channel_id=1, source_target_pairs={{0,16},{1,17},{2,18},{3,19},{4,20},{5,21},{6,22},{7,23},{8,24},{9,... | collective-permute-start | bytes 1671176 | tf_op jit(solution)/shard_map/ppermute | solution.py:31
  202.6 26.7 %collective-permute-start.45 = (bf16[1088,256]{1,0:T(8,128)(2,1)S(1)}, bf16[1088,256]{1,0:T(8,128)(2,1)S(1)}, u32[]{:S(2)}, u32[]{:S(2)}) collective-permute-start(bf16[1088,256]{1,0:T(8,128)(2,1)S(1)} %get-tuple-element.124), channel_id=1, source_target_pairs={{0,48},{1,49},{2,50},{3,51},{4,52},{5,53},{6,54},{7,55},{8,56},{9,... | collective-permute-start | bytes 1671176 | tf_op jit(solution)/shard_map/ppermute | solution.py:31
  216.9 14.7 %collective-permute-start.48 = (bf16[512,256]{1,0:T(8,128)(2,1)S(1)}, bf16[512,256]{1,0:T(8,128)(2,1)S(1)}, u32[]{:S(2)}, u32[]{:S(2)}) collective-permute-start(bf16[512,256]{1,0:T(8,128)(2,1)S(1)} %maximum_select_fusion.1), channel_id=1, source_target_pairs={{0,4},{1,5},{2,6},{3,7},{4,0},{5,1},{6,2},{7,3},{8,12},{9,13},{10,... | collective-permute-start | bytes 786440 | tf_op jit(solution)/shard_map/ppermute | solution.py:36
  (27 other events, 250.0 us)

commit v3 on v2

--- a/solution.py
+++ b/solution.py
@@ -10,8 +10,8 @@
 
 VN = 16
 BS = 128
-UNROLL = 4
-Q_UNROLL = 8
+UNROLL = 16
+Q_UNROLL = 16
 BOTH = ("row", "col")
 MIB = 1 << 20
 F32, BF16 = jnp.float32, jnp.bfloat16
@@ -416,9 +416,10 @@
     weights, pool, other = tie((*agree(weights, pool, other, "y"), other))
     o = scatter_first("row", other)
     own = backward(0, panel)
-    weights, pool, own, o = tie((*agree(weights, pool, (own, o), "zh"), own, o))
+    own, o = tie((own, o))
     terms = scatter_last("row", own, scatter_add(own, other, o))
-    weights = tie(weights.astype(BF16), terms[-1])
+    weights, pool = agree(weights, pool, terms[-1], "zh")
+    weights = weights.astype(BF16)
     for bit in (1, 2):
         weights = merge(weights, "x", x, bit)
     grad_in = weights[:fan].astype(F32).T

time: 234 us -> 224 us (0.957)
  Pallas kernels: 34.5 us -> 26.7 us
  waiting for transfers between devices: 103 us -> 99.3 us
    pallas_call x9, Pallas kernels: 32.3 us -> 24.5 us  [call(): pl.pallas_call(kernel, out_shape=[pltpu.VMEM(shape, dtype) for shape, dty...]
    ppermute x15, starting transfers between devices: 17.2 us -> 20.7 us  [swap(): lax.ppermute(value, BOTH, [(i, i ^ stride * bit) for i in range(128)])]
    ppermute x34, starting transfers between devices: 52.6 us -> 49.1 us  [send(): return lax.ppermute(value, BOTH, route(**step))]
    ppermute x15, waiting for transfers between devices: 26.6 us -> 23.2 us  [swap(): lax.ppermute(value, BOTH, [(i, i ^ stride * bit) for i in range(128)])]
  transfers between devices with their start and end apart: 49 -> 49, of which waited for: 24 -> 25; matrix products, arithmetic and copies ran while one was open for 8% -> 9% of each run, Pallas kernels for 11% -> 9%
where the time goes in v3:
time: 224 us; the launch traced here: 222 us
  waiting for transfers between devices  99.3 us (44%)
  starting transfers between devices  69.9 us (31%)
  Pallas kernels  26.7 us (12%)
  other arithmetic  13.8 us (6%)
  local copies, waits for them, and re-layouts  7.44 us (3%)
  matrix products  3.29 us (1%)
    ppermute x34, waiting for transfers between devices, send(): return lax.ppermute(value, BOTH, route(**step))  76.1 us
    ppermute x34, starting transfers between devices, send(): return lax.ppermute(value, BOTH, route(**step))  49.1 us
    pallas_call x9, Pallas kernels, call(): pl.pallas_call(kernel, out_shape=[pltpu.VMEM(shape, dtype) for shape, dty...  24.5 us
    ppermute x15, waiting for transfers between devices, swap(): lax.ppermute(value, BOTH, [(i, i ^ stride * bit) for i in range(128)])  23.2 us
    ppermute x15, starting transfers between devices, swap(): lax.ppermute(value, BOTH, [(i, i ^ stride * bit) for i in range(128)])  20.7 us
  transfers between devices with their start and end apart: 49, of which 25 were waited for; matrix products, arithmetic and copies ran while one was open for 9% of the time, Pallas kernels for 9%

profile of v3, /device:TPU:1, one launch (start us, length us, event | category | flops | bytes accessed | tf_op | source)
XLA Modules:
  0.0 222.4 jit_solution(16623128499277646397)
XLA Ops:
  0.6 3.8 %collective-permute-start = (bf16[1024,256]{1,0:T(8,128)(2,1)}, bf16[1024,256]{1,0:T(8,128)(2,1)S(1)}, u32[]{:S(2)}, u32[]{:S(2)}) collective-permute-start(bf16[1024,256]{1,0:T(8,128)(2,1)} %bitcast.32), channel_id=1, source_target_pairs={{0,32},{1,33},{2,34},{3,35},{4,36},{5,37},{6,38},{7,39},{8,40},{9,... | collective-permute-start | bytes 1572872 | tf_op jit(solution)/shard_map/ppermute | solution.py:31
  4.5 3.6 %collective-permute-start.7 = (bf16[1024,256]{1,0:T(8,128)(2,1)}, bf16[1024,256]{1,0:T(8,128)(2,1)S(1)}, u32[]{:S(2)}, u32[]{:S(2)}) collective-permute-start(bf16[1024,256]{1,0:T(8,128)(2,1)} %bitcast.33), channel_id=1, source_target_pairs={{0,64},{1,65},{2,66},{3,67},{4,68},{5,69},{6,70},{7,71},{8,72},{9,... | collective-permute-start | bytes 1572872 | tf_op jit(solution)/shard_map/ppermute | solution.py:31
  21.1 2.8 %collective-permute-start.3 = (s32[4,1024]{1,0:T(4,128)S(1)}, s32[4,1024]{1,0:T(4,128)S(1)}, u32[]{:S(2)}, u32[]{:S(2)}) collective-permute-start(s32[4,1024]{1,0:T(4,128)S(1)} %add_select_fusion.2), channel_id=1, source_target_pairs={{0,4},{1,5},{2,6},{3,7},{4,0},{5,1},{6,2},{7,3},{8,12},{9,13},{10,... | collective-permute-start | bytes 49160 | tf_op jit(solution)/shard_map/ppermute | solution.py:36
  26.7 3.2 %stack.13.ends = s32[5]{0:T(128)S(1)} concatenate(s32[1]{0:T(128)} %get-tuple-element.192, s32[1]{0:T(128)} %get-tuple-element.191, s32[1]{0:T(128)} %get-tuple-element.190, s32[1]{0:T(128)} %get-tuple-element.189, s32[1]{0:T(128)} %bitcast.4), dimensions={0} | concatenate | bytes 40 | tf_op jit(solution)/shard_map/stack | solution.py:276
  35.7 4.8 %shard_map.120 = (bf16[32,8192]{1,0:T(8,128)(2,1)S(1)}, bf16[320,128,128]{2,1,0:T(8,128)(2,1)S(1)}) custom-call(s32[320]{0:T(512)S(1)} %get-tuple-element.155.src, s32[320]{0:T(512)S(1)} %get-tuple-element.186.dst, s32[1]{0:T(128)} %bitcast.31.live, bf16[320,128,128]{2,1,0:T(8,128)(2,1)} %bitcast.38, s32[128,1,128]{2,1,0:T(1,128)S(1)} %select_n.380.ids), custom_call_target="tpu_custom_call" | custom-call | flops 167772160 | bytes 10485760 | tf_op jit(solution)/shard_map/pallas_call | solution.py:134
  43.9 3.1 %shard_map.122 = bf16[8192,256]{1,0:T(8,128)(2,1)S(1)} custom-call(s32[288]{0:T(512)S(1)} %get-tuple-element.137.c0, s32[288]{0:T(512)S(1)} %get-tuple-element.136.c1, s32[288]{0:T(512)S(1)} %multiply_add_fusion.to, s32[5]{0:T(128)S(1)} %stack.13.ends, bf16[320,128,128]{2,1,0:T(8,128)(2,1)S(1)} %get-tuple-element.73.adj, ...), custom_call_target="tpu_custom_call" | custom-call | flops 1342177280 | bytes 5242880 | tf_op jit(solution)/shard_map/pallas_call | solution.py:134
  47.0 4.1 %collective-permute-start.13 = (bf16[8192,256]{1,0:T(8,128)(2,1)S(1)}, bf16[8192,256]{1,0:T(8,128)(2,1)S(1)}, u32[]{:S(2)}, u32[]{:S(2)}) collective-permute-start(bf16[8192,256]{1,0:T(8,128)(2,1)S(1)} %shard_map.122), channel_id=1, source_target_pairs={{0,1},{1,0},{2,3},{3,2},{4,5},{5,4},{6,7},{7,6},{8,9},{9,8},{10,11... | collective-permute-start | bytes 12582920 | tf_op jit(solution)/shard_map/ppermute | solution.py:31
  51.1 2.6 %collective-permute-done.11 = f32[16,256]{1,0:T(8,128)S(1)} collective-permute-done((f32[16,256]{1,0:T(8,128)S(1)}, f32[16,256]{1,0:T(8,128)S(1)}, u32[]{:S(2)}, u32[]{:S(2)}) %collective-permute-start.11) | collective-permute-done | bytes 16416 | tf_op jit(solution)/shard_map/ppermute | solution.py:36
  53.7 2.4 %collective-permute-start.12 = (f32[16,256]{1,0:T(8,128)S(1)}, f32[16,256]{1,0:T(8,128)S(1)}, u32[]{:S(2)}, u32[]{:S(2)}) collective-permute-start(f32[16,256]{1,0:T(8,128)S(1)} %add.497), channel_id=1, source_target_pairs={{0,64},{1,65},{2,66},{3,67},{4,68},{5,69},{6,70},{7,71},{8,72},{9,... | collective-permute-start | bytes 49160 | tf_op jit(solution)/shard_map/ppermute | solution.py:36
  65.4 3.1 %collective-permute-start.15 = (f32[16,256]{1,0:T(8,128)S(1)}, f32[16,256]{1,0:T(8,128)S(1)}, u32[]{:S(2)}, u32[]{:S(2)}) collective-permute-start(f32[16,256]{1,0:T(8,128)S(1)} %add.503), channel_id=1, source_target_pairs={{0,32},{1,33},{2,34},{3,35},{4,36},{5,37},{6,38},{7,39},{8,40},{9,... | collective-permute-start | bytes 49160 | tf_op jit(solution)/shard_map/ppermute | solution.py:36
  69.7 4.1 %collective-permute-start.16 = (f32[16,256]{1,0:T(8,128)S(1)}, f32[16,256]{1,0:T(8,128)S(1)}, u32[]{:S(2)}, u32[]{:S(2)}) collective-permute-start(f32[16,256]{1,0:T(8,128)S(1)} %add.504), channel_id=1, source_target_pairs={{0,1},{1,0},{2,3},{3,2},{4,5},{5,4},{6,7},{7,6},{8,9},{9,8},{10,11... | collective-permute-start | bytes 49160 | tf_op jit(solution)/shard_map/ppermute | solution.py:36
  80.5 10.1 %collective-permute-done.20.refs_1_ = bf16[1056,256]{1,0:T(8,128)(2,1)S(1)} collective-permute-done((bf16[1056,256]{1,0:T(8,128)(2,1)S(1)}, bf16[1056,256]{1,0:T(8,128)(2,1)S(1)}, u32[]{:S(2)}, u32[]{:S(2)}) %collective-permute-start.20) | collective-permute-done | bytes 540704 | tf_op jit(solution)/shard_map/ppermute | solution.py:31
  90.6 9.4 %collective-permute-done.21.refs_2_ = bf16[1056,256]{1,0:T(8,128)(2,1)S(1)} collective-permute-done((bf16[1056,256]{1,0:T(8,128)(2,1)S(1)}, bf16[1056,256]{1,0:T(8,128)(2,1)S(1)}, u32[]{:S(2)}, u32[]{:S(2)}) %collective-permute-start.21) | collective-permute-done | bytes 540704 | tf_op jit(solution)/shard_map/ppermute | solution.py:31
  99.9 2.3 %collective-permute-done.22.refs_3_ = bf16[1056,256]{1,0:T(8,128)(2,1)S(1)} collective-permute-done((bf16[1056,256]{1,0:T(8,128)(2,1)S(1)}, bf16[1056,256]{1,0:T(8,128)(2,1)S(1)}, u32[]{:S(2)}, u32[]{:S(2)}) %collective-permute-start.22) | collective-permute-done | bytes 540704 | tf_op jit(solution)/shard_map/ppermute | solution.py:31
  102.3 2.8 %shard_map.125 = (bf16[1024,256]{1,0:T(8,128)(2,1)S(1)}, bf16[1024,512]{1,0:T(8,128)(2,1)S(1)}, bf16[1024,512]{1,0:T(8,128)(2,1)S(1)}, bf16[1024,256]{1,0:T(8,128)(2,1)S(1)}, bf16[32,256]{1,0:T(8,128)(2,1)S(1)}) custom-call(s32[1,1024]{1,0:T(1,128)S(1)} %copy-done.5, f32[16,256]{1,0:T(8,128)S(1)} %fusion.14.pooled, bf16[256,512]{1,0:T(8,128)(2,1)S(1)} %copy-done.4, ...), custom_call_target="tpu_custom_call" | custom-call | flops 805306368 | bytes 2097152 | tf_op jit(solution)/shard_map/pallas_call | solution.py:134
  105.1 3.4 %collective-permute-start.33 = (bf16[1024,256]{1,0:T(8,128)(2,1)S(1)}, bf16[1024,256]{1,0:T(8,128)(2,1)S(1)}, u32[]{:S(2)}, u32[]{:S(2)}) collective-permute-start(bf16[1024,256]{1,0:T(8,128)(2,1)S(1)} %get-tuple-element.92.refs_0_), channel_id=1, source_target_pairs={{0,6},{1,7},{2,0},{3,1},{4,2},{5,3},{6,4},{7,5},{8,14},{9,15},{10,... | collective-permute-start | bytes 1572872 | tf_op jit(solution)/shard_map/ppermute | solution.py:31
  113.3 2.3 %fusion = bf16[1024,256]{1,0:T(8,128)(2,1)} fusion(bf16[1024,512]{1,0:T(8,128)(2,1)S(1)} %get-tuple-element.87, bf16[512,256]{1,0:T(8,128)(2,1)S(1)} %copy-done, bf16[1024,256]{1,0:T(8,128)(2,1)} %copy-done.3), kind=kOutput, calls=%fused_computation.1 | convolution fusion | flops 269221888 | bytes 2359296 | tf_op jit(solution)/shard_map/dot_general | solution.py:115
  115.6 5.6 %collective-permute-done.26.refs_4_ = bf16[1024,256]{1,0:T(8,128)(2,1)S(1)} collective-permute-done((bf16[1024,256]{1,0:T(8,128)(2,1)S(1)}, bf16[1024,256]{1,0:T(8,128)(2,1)S(1)}, u32[]{:S(2)}, u32[]{:S(2)}) %collective-permute-start.26) | collective-permute-done | bytes 524320 | tf_op jit(solution)/shard_map/ppermute | solution.py:31
  121.2 9.2 %collective-permute-done.33.refs_1_ = bf16[1024,256]{1,0:T(8,128)(2,1)S(1)} collective-permute-done((bf16[1024,256]{1,0:T(8,128)(2,1)S(1)}, bf16[1024,256]{1,0:T(8,128)(2,1)S(1)}, u32[]{:S(2)}, u32[]{:S(2)}) %collective-permute-start.33) | collective-permute-done | bytes 524320 | tf_op jit(solution)/shard_map/ppermute | solution.py:31
  130.5 2.4 %collective-permute-done.24 = bf16[1056,256]{1,0:T(8,128)(2,1)} collective-permute-done((bf16[1056,256]{1,0:T(8,128)(2,1)}, bf16[1056,256]{1,0:T(8,128)(2,1)}, u32[]{:S(2)}, u32[]{:S(2)}) %collective-permute-start.24) | collective-permute-done | bytes 540704 | tf_op jit(solution)/shard_map/ppermute | solution.py:36
  135.9 3.2 %collective-permute-done.34.refs_3_ = bf16[1024,256]{1,0:T(8,128)(2,1)S(1)} collective-permute-done((bf16[1024,256]{1,0:T(8,128)(2,1)S(1)}, bf16[1024,256]{1,0:T(8,128)(2,1)S(1)}, u32[]{:S(2)}, u32[]{:S(2)}) %collective-permute-start.34) | collective-permute-done | bytes 524320 | tf_op jit(solution)/shard_map/ppermute | solution.py:31
  141.4 14.3 %collective-permute-done.25 = bf16[288,256]{1,0:T(8,128)(2,1)S(1)} collective-permute-done((bf16[288,256]{1,0:T(8,128)(2,1)S(1)}, bf16[288,256]{1,0:T(8,128)(2,1)S(1)}, u32[]{:S(2)}, u32[]{:S(2)}) %collective-permute-start.25) | collective-permute-done | bytes 147488 | tf_op jit(solution)/shard_map/ppermute | solution.py:31
  161.7 4.1 %shard_map.126 = (bf16[16512,256]{1,0:T(8,128)(2,1)S(1)}, bf16[320,128,128]{2,1,0:T(8,128)(2,1)S(1)}) custom-call(bf16[320,128,128]{2,1,0:T(8,128)(2,1)} %bitcast.39, bf16[1024,256]{1,0:T(8,128)(2,1)S(1)} %get-tuple-element.92.refs_0_, bf16[1024,256]{1,0:T(8,128)(2,1)S(1)} %collective-permute-done.33.refs_1_, ...), custom_call_target="tpu_custom_call" | custom-call | bytes 10485760 | tf_op jit(solution)/shard_map/pallas_call | solution.py:134
  166.8 2.5 %shard_map.127 = (bf16[1088,256]{1,0:T(8,128)(2,1)S(1)}, bf16[1088,256]{1,0:T(8,128)(2,1)S(1)}, bf16[1088,256]{1,0:T(8,128)(2,1)S(1)}, bf16[1088,256]{1,0:T(8,128)(2,1)S(1)}) custom-call(s32[224]{0:T(256)S(1)} %get-tuple-element.139.c0, s32[224]{0:T(256)S(1)} %get-tuple-element.138.c1, s32[224]{0:T(256)S(1)} %multiply_add_fusion.1.to, ...), custom_call_target="tpu_custom_call" | custom-call | flops 1342177280 | bytes 5242880 | tf_op jit(solution)/shard_map/pallas_call | solution.py:134
  173.2 3.3 %collective-permute-start.42 = (bf16[1088,256]{1,0:T(8,128)(2,1)S(1)}, bf16[1088,256]{1,0:T(8,128)(2,1)S(1)}, u32[]{:S(2)}, u32[]{:S(2)}) collective-permute-start(bf16[1088,256]{1,0:T(8,128)(2,1)S(1)} %get-tuple-element.115), channel_id=1, source_target_pairs={{0,64},{1,65},{2,66},{3,67},{4,68},{5,69},{6,70},{7,71},{8,72},{9,... | collective-permute-start | bytes 1671176 | tf_op jit(solution)/shard_map/ppermute | solution.py:31
  178.8 4.7 %collective-permute-done.40 = bf16[1088,256]{1,0:T(8,128)(2,1)S(1)} collective-permute-done((bf16[1088,256]{1,0:T(8,128)(2,1)S(1)}, bf16[1088,256]{1,0:T(8,128)(2,1)S(1)}, u32[]{:S(2)}, u32[]{:S(2)}) %collective-permute-start.40) | collective-permute-done | bytes 557088 | tf_op jit(solution)/shard_map/ppermute | solution.py:31
  183.9 2.6 %collective-permute-done.42 = bf16[1088,256]{1,0:T(8,128)(2,1)S(1)} collective-permute-done((bf16[1088,256]{1,0:T(8,128)(2,1)S(1)}, bf16[1088,256]{1,0:T(8,128)(2,1)S(1)}, u32[]{:S(2)}, u32[]{:S(2)}) %collective-permute-start.42) | collective-permute-done | bytes 557088 | tf_op jit(solution)/shard_map/ppermute | solution.py:31
  186.7 2.8 %collective-permute-start.43 = (bf16[1088,256]{1,0:T(8,128)(2,1)S(1)}, bf16[1088,256]{1,0:T(8,128)(2,1)S(1)}, u32[]{:S(2)}, u32[]{:S(2)}) collective-permute-start(bf16[1088,256]{1,0:T(8,128)(2,1)S(1)} %add_convert_fusion.1), channel_id=1, source_target_pairs={{0,64},{1,65},{2,66},{3,67},{4,68},{5,69},{6,70},{7,71},{8,72},{9,... | collective-permute-start | bytes 1671176 | tf_op jit(solution)/shard_map/ppermute | solution.py:31
  191.8 2.6 %collective-permute-start.46 = (bf16[1088,256]{1,0:T(8,128)(2,1)S(1)}, bf16[1088,256]{1,0:T(8,128)(2,1)S(1)}, u32[]{:S(2)}, u32[]{:S(2)}) collective-permute-start(bf16[1088,256]{1,0:T(8,128)(2,1)S(1)} %get-tuple-element.123), channel_id=1, source_target_pairs={{0,48},{1,49},{2,50},{3,51},{4,52},{5,53},{6,54},{7,55},{8,56},{9,... | collective-permute-start | bytes 1671176 | tf_op jit(solution)/shard_map/ppermute | solution.py:31
  194.4 7.6 %collective-permute-done.39 = bf16[288,256]{1,0:T(8,128)(2,1)S(1)} collective-permute-done((bf16[288,256]{1,0:T(8,128)(2,1)S(1)}, bf16[288,256]{1,0:T(8,128)(2,1)S(1)}, u32[]{:S(2)}, u32[]{:S(2)}) %collective-permute-start.39) | collective-permute-done | bytes 147488 | tf_op jit(solution)/shard_map/ppermute | solution.py:36
  202.2 4.1 %collective-permute-done.47 = bf16[256,256]{1,0:T(8,128)(2,1)S(1)} collective-permute-done((bf16[256,256]{1,0:T(8,128)(2,1)S(1)}, bf16[256,256]{1,0:T(8,128)(2,1)S(1)}, u32[]{:S(2)}, u32[]{:S(2)}) %collective-permute-start.47) | collective-permute-done | bytes 131104 | tf_op jit(solution)/shard_map/ppermute | solution.py:36
  207.7 10.4 %collective-permute-done.44.refs_1_ = bf16[1088,256]{1,0:T(8,128)(2,1)S(1)} collective-permute-done((bf16[1088,256]{1,0:T(8,128)(2,1)S(1)}, bf16[1088,256]{1,0:T(8,128)(2,1)S(1)}, u32[]{:S(2)}, u32[]{:S(2)}) %collective-permute-start.44) | collective-permute-done | bytes 557088 | tf_op jit(solution)/shard_map/ppermute | solution.py:31
  (189 shorter events, 72.9 us)
Async XLA Ops:
  0.6 29.4 %collective-permute-start = (bf16[1024,256]{1,0:T(8,128)(2,1)}, bf16[1024,256]{1,0:T(8,128)(2,1)S(1)}, u32[]{:S(2)}, u32[]{:S(2)}) collective-permute-start(bf16[1024,256]{1,0:T(8,128)(2,1)} %bitcast.32), channel_id=1, source_target_pairs={{0,32},{1,33},{2,34},{3,35},{4,36},{5,37},{6,38},{7,39},{8,40},{9,... | collective-permute-start | bytes 1572872 | tf_op jit(solution)/shard_map/ppermute | solution.py:31
  4.5 26.6 %collective-permute-start.7 = (bf16[1024,256]{1,0:T(8,128)(2,1)}, bf16[1024,256]{1,0:T(8,128)(2,1)S(1)}, u32[]{:S(2)}, u32[]{:S(2)}) collective-permute-start(bf16[1024,256]{1,0:T(8,128)(2,1)} %bitcast.33), channel_id=1, source_target_pairs={{0,64},{1,65},{2,66},{3,67},{4,68},{5,69},{6,70},{7,71},{8,72},{9,... | collective-permute-start | bytes 1572872 | tf_op jit(solution)/shard_map/ppermute | solution.py:31
  8.1 35.0 %collective-permute-start.5 = (bf16[1024,256]{1,0:T(8,128)(2,1)}, bf16[1024,256]{1,0:T(8,128)(2,1)S(1)}, u32[]{:S(2)}, u32[]{:S(2)}) collective-permute-start(bf16[1024,256]{1,0:T(8,128)(2,1)} %bitcast.34), channel_id=1, source_target_pairs={{0,48},{1,49},{2,50},{3,51},{4,52},{5,53},{6,54},{7,55},{8,56},{9,... | collective-permute-start | bytes 1572872 | tf_op jit(solution)/shard_map/ppermute | solution.py:31
  8.8 34.2 %collective-permute-start.6 = (bf16[1024,256]{1,0:T(8,128)(2,1)}, bf16[1024,256]{1,0:T(8,128)(2,1)S(1)}, u32[]{:S(2)}, u32[]{:S(2)}) collective-permute-start(bf16[1024,256]{1,0:T(8,128)(2,1)} %bitcast.35), channel_id=1, source_target_pairs={{0,16},{1,17},{2,18},{3,19},{4,20},{5,21},{6,22},{7,23},{8,24},{9,... | collective-permute-start | bytes 1572872 | tf_op jit(solution)/shard_map/ppermute | solution.py:31
  30.0 12.7 %collective-permute-start.9 = (bf16[1024,256]{1,0:T(8,128)(2,1)S(1)}, bf16[1024,256]{1,0:T(8,128)(2,1)S(1)}, u32[]{:S(2)}, u32[]{:S(2)}) collective-permute-start(bf16[1024,256]{1,0:T(8,128)(2,1)S(1)} %collective-permute-done.refs_2_), channel_id=1, source_target_pairs={{0,64},{1,65},{2,66},{3,67},{4,68},{5,69},{6,70},{7,71},{8,72},{9,... | collective-permute-start | bytes 1572872 | tf_op jit(solution)/shard_map/ppermute | solution.py:31
  31.0 12.1 %collective-permute-start.10 = (bf16[1024,256]{1,0:T(8,128)(2,1)S(1)}, bf16[1024,256]{1,0:T(8,128)(2,1)S(1)}, u32[]{:S(2)}, u32[]{:S(2)}) collective-permute-start(bf16[1024,256]{1,0:T(8,128)(2,1)S(1)} %collective-permute-done.7.refs_4_), channel_id=1, source_target_pairs={{0,16},{1,17},{2,18},{3,19},{4,20},{5,21},{6,22},{7,23},{8,24},{9,... | collective-permute-start | bytes 1572872 | tf_op jit(solution)/shard_map/ppermute | solution.py:31
  58.9 15.8 %collective-permute-start.17 = (bf16[1024,256]{1,0:T(8,128)(2,1)S(1)}, bf16[1024,256]{1,0:T(8,128)(2,1)S(1)}, u32[]{:S(2)}, u32[]{:S(2)}) collective-permute-start(bf16[1024,256]{1,0:T(8,128)(2,1)S(1)} %get-tuple-element.166), channel_id=1, source_target_pairs={{0,2},{1,3},{2,4},{3,5},{4,6},{5,7},{6,0},{7,1},{8,10},{9,11},{10,... | collective-permute-start | bytes 1572872 | tf_op jit(solution)/shard_map/ppermute | solution.py:31
  59.6 15.1 %collective-permute-start.18 = (bf16[1024,256]{1,0:T(8,128)(2,1)S(1)}, bf16[1024,256]{1,0:T(8,128)(2,1)S(1)}, u32[]{:S(2)}, u32[]{:S(2)}) collective-permute-start(bf16[1024,256]{1,0:T(8,128)(2,1)S(1)} %get-tuple-element.164), channel_id=1, source_target_pairs={{0,6},{1,7},{2,0},{3,1},{4,2},{5,3},{6,4},{7,5},{8,14},{9,15},{10,... | collective-permute-start | bytes 1572872 | tf_op jit(solution)/shard_map/ppermute | solution.py:31
  61.6 13.1 %collective-permute-start.19 = (bf16[1024,256]{1,0:T(8,128)(2,1)S(1)}, bf16[1024,256]{1,0:T(8,128)(2,1)S(1)}, u32[]{:S(2)}, u32[]{:S(2)}) collective-permute-start(bf16[1024,256]{1,0:T(8,128)(2,1)S(1)} %get-tuple-element.165), channel_id=1, source_target_pairs={{0,8},{1,9},{2,10},{3,11},{4,12},{5,13},{6,14},{7,15},{8,0},{9,1},... | collective-permute-start | bytes 1572872 | tf_op jit(solution)/shard_map/ppermute | solution.py:31
  75.6 14.9 %collective-permute-start.20 = (bf16[1056,256]{1,0:T(8,128)(2,1)S(1)}, bf16[1056,256]{1,0:T(8,128)(2,1)S(1)}, u32[]{:S(2)}, u32[]{:S(2)}) collective-permute-start(bf16[1056,256]{1,0:T(8,128)(2,1)S(1)} %get-tuple-element.183), channel_id=1, source_target_pairs={{0,2},{1,3},{2,4},{3,5},{4,6},{5,7},{6,0},{7,1},{8,10},{9,11},{10,... | collective-permute-start | bytes 1622024 | tf_op jit(solution)/shard_map/ppermute | solution.py:31
  75.7 24.2 %collective-permute-start.21 = (bf16[1056,256]{1,0:T(8,128)(2,1)S(1)}, bf16[1056,256]{1,0:T(8,128)(2,1)S(1)}, u32[]{:S(2)}, u32[]{:S(2)}) collective-permute-start(bf16[1056,256]{1,0:T(8,128)(2,1)S(1)} %get-tuple-element.182), channel_id=1, source_target_pairs={{0,4},{1,5},{2,6},{3,7},{4,0},{5,1},{6,2},{7,3},{8,12},{9,13},{10,... | collective-permute-start | bytes 1622024 | tf_op jit(solution)/shard_map/ppermute | solution.py:31
  77.7 24.6 %collective-permute-start.22 = (bf16[1056,256]{1,0:T(8,128)(2,1)S(1)}, bf16[1056,256]{1,0:T(8,128)(2,1)S(1)}, u32[]{:S(2)}, u32[]{:S(2)}) collective-permute-start(bf16[1056,256]{1,0:T(8,128)(2,1)S(1)} %get-tuple-element.181), channel_id=1, source_target_pairs={{0,6},{1,7},{2,0},{3,1},{4,2},{5,3},{6,4},{7,5},{8,14},{9,15},{10,... | collective-permute-start | bytes 1622024 | tf_op jit(solution)/shard_map/ppermute | solution.py:31
  79.5 22.7 %collective-permute-start.23 = (bf16[1024,256]{1,0:T(8,128)(2,1)S(1)}, bf16[1024,256]{1,0:T(8,128)(2,1)S(1)}, u32[]{:S(2)}, u32[]{:S(2)}) collective-permute-start(bf16[1024,256]{1,0:T(8,128)(2,1)S(1)} %add_convert_fusion.2), channel_id=1, source_target_pairs={{0,8},{1,9},{2,10},{3,11},{4,12},{5,13},{6,14},{7,15},{8,0},{9,1},... | collective-permute-start | bytes 1572872 | tf_op jit(solution)/shard_map/ppermute | solution.py:31
  105.1 25.3 %collective-permute-start.33 = (bf16[1024,256]{1,0:T(8,128)(2,1)S(1)}, bf16[1024,256]{1,0:T(8,128)(2,1)S(1)}, u32[]{:S(2)}, u32[]{:S(2)}) collective-permute-start(bf16[1024,256]{1,0:T(8,128)(2,1)S(1)} %get-tuple-element.92.refs_0_), channel_id=1, source_target_pairs={{0,6},{1,7},{2,0},{3,1},{4,2},{5,3},{6,4},{7,5},{8,14},{9,15},{10,... | collective-permute-start | bytes 1572872 | tf_op jit(solution)/shard_map/ppermute | solution.py:31
  108.6 12.7 %collective-permute-start.26 = (bf16[1024,256]{1,0:T(8,128)(2,1)S(1)}, bf16[1024,256]{1,0:T(8,128)(2,1)S(1)}, u32[]{:S(2)}, u32[]{:S(2)}) collective-permute-start(bf16[1024,256]{1,0:T(8,128)(2,1)S(1)} %get-tuple-element.92.refs_0_), channel_id=1, source_target_pairs={{0,8},{1,9},{2,10},{3,11},{4,12},{5,13},{6,14},{7,15},{8,0},{9,1},... | collective-permute-start | bytes 1572872 | tf_op jit(solution)/shard_map/ppermute | solution.py:31
  112.1 20.8 %collective-permute-start.24 = (bf16[1056,256]{1,0:T(8,128)(2,1)}, bf16[1056,256]{1,0:T(8,128)(2,1)}, u32[]{:S(2)}, u32[]{:S(2)}) collective-permute-start(bf16[1056,256]{1,0:T(8,128)(2,1)} %pad_maximum_fusion.13), channel_id=1, source_target_pairs={{0,8},{1,9},{2,10},{3,11},{4,12},{5,13},{6,14},{7,15},{8,0},{9,1},... | collective-permute-start | bytes 1622024 | tf_op jit(solution)/shard_map/ppermute | solution.py:36
  112.6 21.6 %collective-permute-start.29 = (bf16[1024,256]{1,0:T(8,128)(2,1)S(1)}, bf16[1024,256]{1,0:T(8,128)(2,1)S(1)}, u32[]{:S(2)}, u32[]{:S(2)}) collective-permute-start(bf16[1024,256]{1,0:T(8,128)(2,1)S(1)} %get-tuple-element.92.refs_0_), channel_id=1, source_target_pairs={{0,4},{1,5},{2,6},{3,7},{4,0},{5,1},{6,2},{7,3},{8,12},{9,13},{10,... | collective-permute-start | bytes 1572872 | tf_op jit(solution)/shard_map/ppermute | solution.py:31
  112.9 26.3 %collective-permute-start.34 = (bf16[1024,256]{1,0:T(8,128)(2,1)S(1)}, bf16[1024,256]{1,0:T(8,128)(2,1)S(1)}, u32[]{:S(2)}, u32[]{:S(2)}) collective-permute-start(bf16[1024,256]{1,0:T(8,128)(2,1)S(1)} %get-tuple-element.92.refs_0_), channel_id=1, source_target_pairs={{0,2},{1,3},{2,4},{3,5},{4,6},{5,7},{6,0},{7,1},{8,10},{9,11},{10,... | collective-permute-start | bytes 1572872 | tf_op jit(solution)/shard_map/ppermute | solution.py:31
  134.3 21.3 %collective-permute-start.27 = (bf16[1312,256]{1,0:T(8,128)(2,1)S(1)}, bf16[1312,256]{1,0:T(8,128)(2,1)S(1)}, u32[]{:S(2)}, u32[]{:S(2)}) collective-permute-start(bf16[1312,256]{1,0:T(8,128)(2,1)S(1)} %get-tuple-element.168), channel_id=1, source_target_pairs={{0,6},{1,7},{2,0},{3,1},{4,2},{5,3},{6,4},{7,5},{8,14},{9,15},{10,... | collective-permute-start | bytes 2015240 | tf_op jit(solution)/shard_map/ppermute | solution.py:31
  135.6 20.1 %collective-permute-start.28 = (bf16[1312,256]{1,0:T(8,128)(2,1)S(1)}, bf16[1312,256]{1,0:T(8,128)(2,1)S(1)}, u32[]{:S(2)}, u32[]{:S(2)}) collective-permute-start(bf16[1312,256]{1,0:T(8,128)(2,1)S(1)} %get-tuple-element.169), channel_id=1, source_target_pairs={{0,2},{1,3},{2,4},{3,5},{4,6},{5,7},{6,0},{7,1},{8,10},{9,11},{10,... | collective-permute-start | bytes 2015240 | tf_op jit(solution)/shard_map/ppermute | solution.py:31
  139.2 22.5 %collective-permute-start.35 = (bf16[5120,256]{1,0:T(8,128)(2,1)S(1)}, bf16[5120,256]{1,0:T(8,128)(2,1)S(1)}, u32[]{:S(2)}, u32[]{:S(2)}) collective-permute-start(bf16[5120,256]{1,0:T(8,128)(2,1)S(1)} %constant_dynamic-update-slice_fusion), channel_id=1, source_target_pairs={{0,1},{1,0},{2,3},{3,2},{4,5},{5,4},{6,7},{7,6},{8,9},{9,8},{10,11... | collective-permute-start | bytes 7864328 | tf_op jit(solution)/shard_map/ppermute | solution.py:31
  139.8 15.8 %collective-permute-start.25 = (bf16[288,256]{1,0:T(8,128)(2,1)S(1)}, bf16[288,256]{1,0:T(8,128)(2,1)S(1)}, u32[]{:S(2)}, u32[]{:S(2)}) collective-permute-start(bf16[288,256]{1,0:T(8,128)(2,1)S(1)} %pad_maximum_fusion.14), channel_id=1, source_target_pairs={{0,4},{1,5},{2,6},{3,7},{4,0},{5,1},{6,2},{7,3},{8,12},{9,13},{10,... | collective-permute-start | bytes 442376 | tf_op jit(solution)/shard_map/ppermute | solution.py:31
  140.4 15.4 %collective-permute-start.30 = (bf16[1024,256]{1,0:T(8,128)(2,1)S(1)}, bf16[1024,256]{1,0:T(8,128)(2,1)S(1)}, u32[]{:S(2)}, u32[]{:S(2)}) collective-permute-start(bf16[1024,256]{1,0:T(8,128)(2,1)S(1)} %collective-permute-done.29.refs_2_), channel_id=1, source_target_pairs={{0,8},{1,9},{2,10},{3,11},{4,12},{5,13},{6,14},{7,15},{8,0},{9,1},... | collective-permute-start | bytes 1572872 | tf_op jit(solution)/shard_map/ppermute | solution.py:31
  170.4 13.0 %collective-permute-start.40 = (bf16[1088,256]{1,0:T(8,128)(2,1)S(1)}, bf16[1088,256]{1,0:T(8,128)(2,1)S(1)}, u32[]{:S(2)}, u32[]{:S(2)}) collective-permute-start(bf16[1088,256]{1,0:T(8,128)(2,1)S(1)} %get-tuple-element.113), channel_id=1, source_target_pairs={{0,16},{1,17},{2,18},{3,19},{4,20},{5,21},{6,22},{7,23},{8,24},{9,... | collective-permute-start | bytes 1671176 | tf_op jit(solution)/shard_map/ppermute | solution.py:31
  171.2 12.7 %collective-permute-start.41 = (bf16[1088,256]{1,0:T(8,128)(2,1)S(1)}, bf16[1088,256]{1,0:T(8,128)(2,1)S(1)}, u32[]{:S(2)}, u32[]{:S(2)}) collective-permute-start(bf16[1088,256]{1,0:T(8,128)(2,1)S(1)} %get-tuple-element.114), channel_id=1, source_target_pairs={{0,48},{1,49},{2,50},{3,51},{4,52},{5,53},{6,54},{7,55},{8,56},{9,... | collective-permute-start | bytes 1671176 | tf_op jit(solution)/shard_map/ppermute | solution.py:31
  173.2 13.3 %collective-permute-start.42 = (bf16[1088,256]{1,0:T(8,128)(2,1)S(1)}, bf16[1088,256]{1,0:T(8,128)(2,1)S(1)}, u32[]{:S(2)}, u32[]{:S(2)}) collective-permute-start(bf16[1088,256]{1,0:T(8,128)(2,1)S(1)} %get-tuple-element.115), channel_id=1, source_target_pairs={{0,64},{1,65},{2,66},{3,67},{4,68},{5,69},{6,70},{7,71},{8,72},{9,... | collective-permute-start | bytes 1671176 | tf_op jit(solution)/shard_map/ppermute | solution.py:31
  186.7 15.3 %collective-permute-start.43 = (bf16[1088,256]{1,0:T(8,128)(2,1)S(1)}, bf16[1088,256]{1,0:T(8,128)(2,1)S(1)}, u32[]{:S(2)}, u32[]{:S(2)}) collective-permute-start(bf16[1088,256]{1,0:T(8,128)(2,1)S(1)} %add_convert_fusion.1), channel_id=1, source_target_pairs={{0,64},{1,65},{2,66},{3,67},{4,68},{5,69},{6,70},{7,71},{8,72},{9,... | collective-permute-start | bytes 1671176 | tf_op jit(solution)/shard_map/ppermute | solution.py:31
  189.5 12.5 %collective-permute-start.39 = (bf16[288,256]{1,0:T(8,128)(2,1)S(1)}, bf16[288,256]{1,0:T(8,128)(2,1)S(1)}, u32[]{:S(2)}, u32[]{:S(2)}) collective-permute-start(bf16[288,256]{1,0:T(8,128)(2,1)S(1)} %pad_maximum_fusion.20), channel_id=1, source_target_pairs={{0,64},{1,65},{2,66},{3,67},{4,68},{5,69},{6,70},{7,71},{8,72},{9,... | collective-permute-start | bytes 442376 | tf_op jit(solution)/shard_map/ppermute | solution.py:36
  190.0 17.7 %collective-permute-start.45 = (bf16[1088,256]{1,0:T(8,128)(2,1)S(1)}, bf16[1088,256]{1,0:T(8,128)(2,1)S(1)}, u32[]{:S(2)}, u32[]{:S(2)}) collective-permute-start(bf16[1088,256]{1,0:T(8,128)(2,1)S(1)} %add_convert_fusion), channel_id=1, source_target_pairs={{0,32},{1,33},{2,34},{3,35},{4,36},{5,37},{6,38},{7,39},{8,40},{9,... | collective-permute-start | bytes 1671176 | tf_op jit(solution)/shard_map/ppermute | solution.py:31
  191.8 26.3 %collective-permute-start.44 = (bf16[1088,256]{1,0:T(8,128)(2,1)S(1)}, bf16[1088,256]{1,0:T(8,128)(2,1)S(1)}, u32[]{:S(2)}, u32[]{:S(2)}) collective-permute-start(bf16[1088,256]{1,0:T(8,128)(2,1)S(1)} %get-tuple-element.120), channel_id=1, source_target_pairs={{0,16},{1,17},{2,18},{3,19},{4,20},{5,21},{6,22},{7,23},{8,24},{9,... | collective-permute-start | bytes 1671176 | tf_op jit(solution)/shard_map/ppermute | solution.py:31
  191.8 26.3 %collective-permute-start.46 = (bf16[1088,256]{1,0:T(8,128)(2,1)S(1)}, bf16[1088,256]{1,0:T(8,128)(2,1)S(1)}, u32[]{:S(2)}, u32[]{:S(2)}) collective-permute-start(bf16[1088,256]{1,0:T(8,128)(2,1)S(1)} %get-tuple-element.123), channel_id=1, source_target_pairs={{0,48},{1,49},{2,50},{3,51},{4,52},{5,53},{6,54},{7,55},{8,56},{9,... | collective-permute-start | bytes 1671176 | tf_op jit(solution)/shard_map/ppermute | solution.py:31
  206.4 13.9 %collective-permute-start.48 = (bf16[512,256]{1,0:T(8,128)(2,1)S(1)}, bf16[512,256]{1,0:T(8,128)(2,1)S(1)}, u32[]{:S(2)}, u32[]{:S(2)}) collective-permute-start(bf16[512,256]{1,0:T(8,128)(2,1)S(1)} %maximum_select_fusion.1), channel_id=1, source_target_pairs={{0,4},{1,5},{2,6},{3,7},{4,0},{5,1},{6,2},{7,3},{8,12},{9,13},{10,... | collective-permute-start | bytes 786440 | tf_op jit(solution)/shard_map/ppermute | solution.py:36
  (27 other events, 249.9 us)
